TPU v7x, 256 devices: a whole 4x4x8 slice. The times are simulated.
256 devices in a mesh: section: 2 (over x_lo), seq: 16 (over z, x_hi), tp: 8 (over y, core).
Axes of the slice: x: 4 (x_hi: 2, x_lo: 2; x = x_hi * 2 + x_lo), y: 4, z: 8, core: 2. Of those that a mesh axis runs over, the one named last changes fastest.
Arguments:
- layer_input: bfloat16 [2, 4096, 8192], P('section', 'seq', 'tp'), may hold values from -200 to 200, as said below
- norm_gain: float32 [2, 8192], P('section', 'tp'), may hold values from 0.1 to 1.9
- kv_cotangent: bfloat16 [2, 4096, 2048], P('section', 'seq', 'tp'), may hold values from -8 to 8
- kv_weight: bfloat16 [2, 2048, 8192], P('section', 'tp', 'seq'), may hold values from -0.09375 to 0.09375
- mlp_grads: bfloat16 [2, 4096, 8192], P('section', 'seq', 'tp'), may hold values from -6 to 6
- output_cotangent: bfloat16 [4096, 8192], P('seq', 'tp'), may hold values from -6 to 6
- out_weight: bfloat16 [2, 8192, 8192], P('section', 'tp', 'seq'), may hold values from -0.0625 to 0.0625
Outputs:
- attn_grads: bfloat16 [2, 4096, 8192], P('section', 'seq', 'tp')
- input_grads: bfloat16 [2, 4096, 8192], P('section', 'seq', 'tp')
Inputs may be any that keep to these rules, and one draw needn't show every extreme that they name: `layer_input`: real-valued activations.
All inputs are finite; a program needn't handle non-finite values.
Results may differ from a plain program's by a relative error of at most 0.0055.
Values may be sent and summed in bfloat16 or wider, within the bound.
A program may use at most 128 MiB of HBM per device.

v0:
```python
import jax
import jax.numpy as jnp
from jax import lax
from jax.sharding import PartitionSpec as P

D = 8192


epsilon = 1e-05


def from_behind(block, axis, distance):
    devices = range(lax.axis_size(axis))
    route = [(i - distance, i) for i in devices if i - distance in devices]
    return lax.ppermute(block, axis, route)


def body(layer_input, norm_gain, kv_cotangent, kv_weight, mlp_grads, output_cotangent, out_weight):
    section_index = lax.axis_index("section")
    values = layer_input[0].astype(jnp.float32)
    gain = norm_gain[0]
    cotangent = kv_cotangent[0]
    kv_terms = jnp.dot(
        cotangent,
        lax.all_gather(kv_weight[0], "seq", axis=1, tiled=True),
        preferred_element_type=jnp.float32,
    )
    kv_share = lax.psum_scatter(kv_terms, "tp", scatter_dimension=1, tiled=True)
    squares, intersection = lax.psum(
        (jnp.sum(values * values, axis=1), jnp.sum(gain * kv_share * values, axis=1)), "tp"
    )
    inv_rms = lax.rsqrt(squares / D + epsilon)[:, None]
    norm_back = (
        inv_rms * gain * kv_share
        - values * (inv_rms * inv_rms * inv_rms) * intersection[:, None] / D
    )
    branch = mlp_grads[0].astype(jnp.float32)
    grad_one = output_cotangent.astype(jnp.float32) + branch
    input_one = (grad_one + norm_back).astype(jnp.bfloat16)
    arriving = from_behind(input_one, "section", -1)
    grad_zero = arriving.astype(jnp.float32) + branch
    upstream = section_index == 0
    input_part = jnp.where(upstream, (grad_zero + norm_back).astype(jnp.bfloat16), input_one)
    grad_cast = jnp.where(upstream, grad_zero, grad_one).astype(jnp.bfloat16)
    grad_full = lax.all_gather(grad_cast, "tp", axis=1, tiled=True)
    attn_part = lax.dot_general(
        grad_full,
        lax.all_gather(out_weight[0], "seq", axis=1, tiled=True),
        (((1,), (1,)), ((), ())),
        preferred_element_type=jnp.float32,
    )
    return (attn_part.astype(jnp.bfloat16)[None], input_part[None])


def solution(mesh):
    in_specs = (
        P("section", "seq", "tp"),
        P("section", "tp"),
        P("section", "seq", "tp"),
        P("section", "tp", "seq"),
        P("section", "seq", "tp"),
        P("seq", "tp"),
        P("section", "tp", "seq"),
    )
    out_specs = (P("section", "seq", "tp"), P("section", "seq", "tp"))
    return jax.shard_map(body, mesh=mesh, in_specs=in_specs, out_specs=out_specs, check_vma=False)
```

profile of v0, /device:TPU:2, one launch (start us, length us, event | category | flops | bytes accessed | tf_op | source)
XLA Modules:
  0.0 480.9 jit_solution(13414301139008872900)
XLA Ops:
  7.2 0.0 copy-start
  7.2 0.0 all-gather.8.cloned.1.call-start
  7.2 0.7 all-gather.8.cloned.1.call-update
  7.9 0.0 reduce-scatter.2.cloned.1.call-start
  8.0 109.9 %all-gather.8.cloned.1.call-done = bf16[1,256,8192]{2,1,0:T(8,128)(2,1)} async-done(((bf16[1,256,512]{2,1,0:T(8,128)(2,1)}), bf16[1,256,8192]{2,1,0:T(8,128)(2,1)}) %all-gather.8.cloned.1.call-update) | async-done | bytes 4194320 | tf_op jit(solution)/shard_map/all_gather | solution.py:25
  117.9 0.0 copy-done
  117.9 6.7 %fusion.2 = f32[256,8192]{1,0:T(8,128)} fusion(bf16[1,256,8192]{2,1,0:T(8,128)(2,1)} %all-gather.8.cloned.1.call-done, bf16[1,256,256]{2,1,0:T(8,128)(2,1)S(1)} %copy-done), kind=kOutput, calls=%fused_computation.2 | convolution fusion | flops 1073741824 | bytes 12713984 | tf_op jit(solution)/shard_map/dot_general | solution.py:23
  124.6 0.0 reduce-scatter.2.cloned.1.call-update
  124.6 0.0 all-gather.10.cloned.1.call-start
  124.6 0.7 all-gather.10.cloned.1.call-update
  125.3 0.0 all-gather.6.cloned.1.call-start
  125.4 51.8 %reduce-scatter.2.cloned.1.call-done = f32[256,1024]{1,0:T(8,128)} async-done(((f32[256,8192]{1,0:T(8,128)}), f32[256,1024]{1,0:T(8,128)}) %reduce-scatter.2.cloned.1.call-update) | async-done | bytes 1048592 | tf_op jit(solution)/shard_map/reduce_scatter | solution.py:28
  177.2 1.6 fusion.10
  178.8 12.8 %all-reduce = (f32[256]{0:T(256)S(1)}, f32[256]{0:T(256)S(1)}) all-reduce(f32[256]{0:T(256)S(1)} %get-tuple-element.3, f32[256]{0:T(256)S(1)} %get-tuple-element.2), channel_id=1, replica_groups=mesh['section'=2,'seq'=16,'tp'=8] {'tp'}, use_global_device_ids=true, to_apply=%region_4.0 | all-reduce | flops 512 | bytes 4096 | tf_op jit(solution)/shard_map/psum | solution.py:29
  191.7 0.0 copy-done.2
  191.7 2.6 add_convert_fusion.1
  194.3 2.6 collective-permute-start
  196.9 18.6 %collective-permute-done = bf16[256,1024]{1,0:T(8,128)(2,1)S(1)} collective-permute-done((bf16[256,1024]{1,0:T(8,128)(2,1)}, bf16[256,1024]{1,0:T(8,128)(2,1)S(1)}, u32[]{:S(2)}, u32[]{:S(2)}) %collective-permute-start) | collective-permute-done | bytes 524320 | tf_op jit(solution)/shard_map/ppermute | solution.py:15
  215.5 1.1 select_convert_fusion
  216.6 0.0 all-gather.6.cloned.1.call-update
  216.6 1.4 fusion.16
  218.0 209.6 %all-gather.10.cloned.1.call-done = bf16[1,1024,8192]{2,1,0:T(8,128)(2,1)} async-done(((bf16[1,1024,512]{2,1,0:T(8,128)(2,1)}), bf16[1,1024,8192]{2,1,0:T(8,128)(2,1)}) %all-gather.10.cloned.1.call-update) | async-done | bytes 16777232 | tf_op jit(solution)/shard_map/all_gather | solution.py:48
  427.6 34.4 %all-gather.6.cloned.1.call-done = bf16[256,8192]{1,0:T(8,128)(2,1)} async-done(((bf16[256,1024]{1,0:T(8,128)(2,1)}), bf16[256,8192]{1,0:T(8,128)(2,1)}) %all-gather.6.cloned.1.call-update) | async-done | bytes 4194320 | tf_op jit(solution)/shard_map/all_gather | solution.py:45
  462.0 12.4 %fusion.7 = bf16[1,256,1024]{2,1,0:T(8,128)(2,1)} fusion(bf16[256,8192]{1,0:T(8,128)(2,1)} %all-gather.6.cloned.1.call-done, bf16[1,1024,8192]{2,1,0:T(8,128)(2,1)} %all-gather.10.cloned.1.call-done), kind=kOutput, calls=%fused_computation.10 | convolution fusion | flops 4295229440 | bytes 21495808 | tf_op jit(solution)/shard_map/dot_general | solution.py:46
  (10 shorter events, 0.0 us)
Async XLA Ops:
  7.2 110.7 %copy-start = (bf16[1,256,256]{2,1,0:T(8,128)(2,1)S(1)}, bf16[1,256,256]{2,1,0:T(8,128)(2,1)}, u32[]{:S(2)}) copy-start(bf16[1,256,256]{2,1,0:T(8,128)(2,1)} %param.9) | copy-start | bytes 393220
  7.2 110.7 %all-gather.8.cloned.1.call-start = ((), (), s32[]{:S(2)}) async-start(), calls=%async_computation.3 | async-start | bytes 4456448 | tf_op jit(solution)/shard_map/all_gather | solution.py:25
  7.9 169.3 %reduce-scatter.2.cloned.1.call-start = ((), (), s32[]{:S(2)}) async-start(), calls=%async_computation.1 | async-start | bytes 9437184 | tf_op jit(solution)/shard_map/reduce_scatter | solution.py:28
  124.6 52.6 %copy-start.4 = (bf16[1,256,1024]{2,1,0:T(8,128)(2,1)S(1)}, bf16[1,256,1024]{2,1,0:T(8,128)(2,1)}, u32[]{:S(2)}) copy-start(bf16[1,256,1024]{2,1,0:T(8,128)(2,1)} %param.7) | copy-start | bytes 1572868
  124.6 52.6 %copy-start.5 = (f32[1,1024]{1,0:T(1,128)S(1)}, f32[1,1024]{1,0:T(1,128)}, u32[]{:S(2)}) copy-start(f32[1,1024]{1,0:T(1,128)} %param.8) | copy-start | bytes 12292
  124.6 67.1 %copy-start.2 = (bf16[256,1024]{1,0:T(8,128)(2,1)S(1)}, bf16[256,1024]{1,0:T(8,128)(2,1)}, u32[]{:S(2)}) copy-start(bf16[256,1024]{1,0:T(8,128)(2,1)} %param.12) | copy-start | bytes 1572868
  124.6 67.1 %copy-start.3 = (bf16[1,256,1024]{2,1,0:T(8,128)(2,1)S(1)}, bf16[1,256,1024]{2,1,0:T(8,128)(2,1)}, u32[]{:S(2)}) copy-start(bf16[1,256,1024]{2,1,0:T(8,128)(2,1)} %param.11) | copy-start | bytes 1572868
  124.6 303.0 %all-gather.10.cloned.1.call-start = ((), (), s32[]{:S(2)}) async-start(), calls=%async_computation.4 | async-start | bytes 17825792 | tf_op jit(solution)/shard_map/all_gather | solution.py:48
  125.3 336.7 %all-gather.6.cloned.1.call-start = ((), (), s32[]{:S(2)}) async-start(), calls=%async_computation.2 | async-start | bytes 4718592 | tf_op jit(solution)/shard_map/all_gather | solution.py:45
  177.2 39.4 %copy-start.1 = (f32[256,1024]{1,0:T(8,128)S(1)}, f32[256,1024]{1,0:T(8,128)}, u32[]{:S(2)}) copy-start(f32[256,1024]{1,0:T(8,128)} %reduce-scatter.2.cloned.1.call-done) | copy-start | bytes 3145732
  194.3 21.2 %collective-permute-start = (bf16[256,1024]{1,0:T(8,128)(2,1)}, bf16[256,1024]{1,0:T(8,128)(2,1)S(1)}, u32[]{:S(2)}, u32[]{:S(2)}) collective-permute-start(bf16[256,1024]{1,0:T(8,128)(2,1)} %add_convert_fusion.1), channel_id=1, source_target_pairs={{128,0},{129,1},{130,2},{131,3},{132,4},{133,5},{134,6},{135,7},{1... | collective-permute-start | bytes 1572872 | tf_op jit(solution)/shard_map/ppermute | solution.py:15
Sparse Core Ops, SparseCore 0:
  10.5 107.3 all-gather.7
  124.7 52.4 reduce-scatter.1
  179.7 247.8 all-gather.9
  429.9 32.0 all-gather.5
where the time goes:
time: 482 us; the launch traced here: 481 us
  waiting for transfers between devices  426 us (88%)
  matrix products  19 us (4%)
  between operations  13.8 us (3%)
  blocking collectives  12.8 us (3%)
  other arithmetic  6.67 us (1%)
    all_gather x1, waiting for transfers between devices, body(): lax.all_gather(out_weight[0], 'seq', axis=1, tiled=True)  210 us
    all_gather x1, waiting for transfers between devices, body(): lax.all_gather(kv_weight[0], 'seq', axis=1, tiled=True)  110 us
    reduce_scatter x1, waiting for transfers between devices, body(): kv_share = lax.psum_scatter(kv_terms, 'tp', scatter_dimension=1, tiled=True)  51.8 us
    all_gather x1, waiting for transfers between devices, body(): grad_full = lax.all_gather(grad_cast, 'tp', axis=1, tiled=True)  34.4 us
    ppermute x1, waiting for transfers between devices, from_behind(): return lax.ppermute(block, axis, route)  18.6 us
    psum x1, blocking collectives, body(): lax.psum((jnp.sum(values * values, axis=1), jnp.sum(gain * kv_share * val...  12.8 us
    dot_general x1, matrix products, body(): lax.dot_general(grad_full, lax.all_gather(out_weight[0], 'seq', axis=1, t...  12.4 us
  transfers between devices with their start and end apart: 5, of which 5 were waited for; matrix products, arithmetic and copies ran while one was open for 1% of the time, Pallas kernels for 0%

commit v1 on v0

v1 whole, which is shorter than its diff:
```python
import jax
import jax.numpy as jnp
from jax import lax
from jax.sharding import Mesh, PartitionSpec as P

D = 8192
epsilon = 1e-05
SEQ = ("z", "xh")


def body(layer_input, norm_gain, kv_cotangent, kv_weight, mlp_grads, output_cotangent, out_weight):
    section_index = lax.axis_index("section")
    h = lax.axis_index("xh")
    swap = [(0, 1), (1, 0)]
    values = layer_input[0].astype(jnp.float32)
    gain = norm_gain[0]
    squares = jnp.sum(values * values, axis=1)
    kvw = lax.all_gather(kv_weight[0], "z", axis=0)
    kvw = lax.all_to_all(kvw, "tp", 0, 0, tiled=True).reshape(2048, 512)
    out_w = lax.all_gather(out_weight[0], "z", axis=0)
    mine = kv_cotangent[0]
    theirs = lax.ppermute(mine, "xh", swap)
    cot = jnp.stack([mine, theirs])
    cot = lax.all_gather(cot, "tp", axis=2, tiled=True)
    terms_own = jnp.dot(cot[0], kvw, preferred_element_type=jnp.float32)
    terms_their = jnp.dot(cot[1], kvw, preferred_element_type=jnp.float32).astype(jnp.bfloat16)
    arrived = lax.ppermute(terms_their, "xh", swap).astype(jnp.float32)
    kv_share = jnp.where(
        h == 0,
        jnp.concatenate([terms_own, arrived], axis=1),
        jnp.concatenate([arrived, terms_own], axis=1),
    )
    squares, intersection = lax.psum((squares, jnp.sum(gain * kv_share * values, axis=1)), "tp")
    inv_rms = lax.rsqrt(squares / D + epsilon)[:, None]
    norm_back = (
        inv_rms * gain * kv_share
        - values * (inv_rms * inv_rms * inv_rms) * intersection[:, None] / D
    )
    branch = mlp_grads[0].astype(jnp.float32)
    grad_one = output_cotangent.astype(jnp.float32) + branch
    input_one = (grad_one + norm_back).astype(jnp.bfloat16)
    arriving = lax.ppermute(input_one, "section", [(1, 0)])
    grad_zero = arriving.astype(jnp.float32) + branch
    upstream = section_index == 0
    input_part = jnp.where(upstream, (grad_zero + norm_back).astype(jnp.bfloat16), input_one)
    grad_cast = jnp.where(upstream, grad_zero, grad_one).astype(jnp.bfloat16)
    left, right = grad_cast[:, :512], grad_cast[:, 512:]
    keep = jnp.where(h == 0, left, right)
    give = jnp.where(h == 0, right, left)
    got = lax.ppermute(give, "xh", swap)
    pair = lax.all_gather(jnp.stack([keep, got]), "tp", axis=0)
    parts = lax.dot_general(
        pair.transpose(1, 2, 0, 3).reshape(512, 4096),
        out_w.transpose(1, 0, 2).reshape(1024, 4096),
        (((1,), (1,)), ((), ())),
        preferred_element_type=jnp.float32,
    )
    other = lax.ppermute(parts[256:].astype(jnp.bfloat16), "xh", swap)
    attn = parts[:256] + other.astype(jnp.float32)
    return (attn.astype(jnp.bfloat16)[None], input_part[None])


def solution(mesh):
    seq = mesh.shape["seq"]
    fine = Mesh(
        mesh.devices.reshape(mesh.shape["section"], seq // 2, 2, mesh.shape["tp"]),
        ("section", "z", "xh", "tp"),
    )
    in_specs = (
        P("section", SEQ, "tp"),
        P("section", "tp"),
        P("section", SEQ, "tp"),
        P("section", "tp", SEQ),
        P("section", SEQ, "tp"),
        P(SEQ, "tp"),
        P("section", "tp", SEQ),
    )
    out_specs = (P("section", SEQ, "tp"), P("section", SEQ, "tp"))
    return jax.shard_map(body, mesh=fine, in_specs=in_specs, out_specs=out_specs, check_vma=False)
```

time: 482 us -> 320 us (0.66)
  waiting for transfers between devices: 426 us -> 236 us
  local copies, waits for them, and re-layouts: 0.03 us -> 21.6 us
  starting transfers between devices: 2.78 us -> 16 us
  matrix products: 19 us -> 12.4 us
    all_gather x3 -> x4, waiting for transfers between devices: 354 us -> 195 us  [the longest x1 87.1 us: body(): out_w = lax.all_gather(out_weight[0], 'z', axis=0)]
    reduce_scatter x1 -> x0, waiting for transfers between devices: 51.8 us -> none  [body(): kv_share = lax.psum_scatter(kv_terms, 'tp', scatter_dimension=1, tiled=True)]
    ppermute x1 -> x5, waiting for transfers between devices: 18.6 us -> 39.7 us  [the longest x1 11.7 us: body(): other = lax.ppermute(parts[256:].astype(jnp.bfloat16), 'xh', swap)]
    all_gather x0 -> x2, local copies, waits for them, and re-layouts: none -> 16 us  [the longest x1 11.5 us: body(): out_w = lax.all_gather(out_weight[0], 'z', axis=0)]
    ppermute x1 -> x5, starting transfers between devices: 2.63 us -> 11.5 us  [the longest x1 2.49 us: body(): arriving = lax.ppermute(input_one, 'section', [(1, 0)])]
    dot_general x2 -> x3, matrix products: 19 us -> 12.4 us  [the longest x1 8.14 us: body(): lax.dot_general(pair.transpose(1, 2, 0, 3).reshape(512, 4096), out_w.tran...]
    unnamed x12 -> x13, local copies, waits for them, and re-layouts: 0.03 us -> 5.51 us
  transfers between devices with their start and end apart: 5 -> 10, of which waited for: 5 -> 9; matrix products, arithmetic and copies ran while one was open for 1% -> 4% of each run, Pallas kernels for 0% -> 0%
where the time goes in v1:
time: 320 us; the launch traced here: 319 us
  waiting for transfers between devices  236 us (74%)
  local copies, waits for them, and re-layouts  21.6 us (7%)
  starting transfers between devices  16 us (5%)
  between operations  13.9 us (4%)
  blocking collectives  12.5 us (4%)
  matrix products  12.4 us (4%)
  other arithmetic  6.78 us (2%)
    all_gather x1, waiting for transfers between devices, body(): out_w = lax.all_gather(out_weight[0], 'z', axis=0)  87.1 us
    all_gather x1, waiting for transfers between devices, body(): cot = lax.all_gather(cot, 'tp', axis=2, tiled=True)  37.3 us
    all_gather x1, waiting for transfers between devices, body(): kvw = lax.all_gather(kv_weight[0], 'z', axis=0)  37.2 us
    all_gather x1, waiting for transfers between devices, body(): pair = lax.all_gather(jnp.stack([keep, got]), 'tp', axis=0)  33.4 us
    psum x1, blocking collectives, body(): lax.psum((squares, jnp.sum(gain * kv_share * values, axis=1)), 'tp')  12.5 us
    ppermute x1, waiting for transfers between devices, body(): other = lax.ppermute(parts[256:].astype(jnp.bfloat16), 'xh', swap)  11.7 us
    all_gather x1, local copies, waits for them, and re-layouts, body(): out_w = lax.all_gather(out_weight[0], 'z', axis=0)  11.5 us
    ppermute x1, waiting for transfers between devices, body(): arriving = lax.ppermute(input_one, 'section', [(1, 0)])  11.4 us
  transfers between devices with their start and end apart: 10, of which 9 were waited for; matrix products, arithmetic and copies ran while one was open for 4% of the time, Pallas kernels for 0%

profile of v1, /device:TPU:2, one launch (start us, length us, event | category | flops | bytes accessed | tf_op | source)
XLA Modules:
  0.0 319.0 jit_solution(3558069060889546405)
XLA Ops:
  7.9 2.2 collective-permute-start
  10.2 4.8 %collective-permute-done = bf16[256,256]{1,0:T(8,128)(2,1)S(1)} collective-permute-done((bf16[256,256]{1,0:T(8,128)(2,1)}, bf16[256,256]{1,0:T(8,128)(2,1)S(1)}, u32[]{:S(2)}, u32[]{:S(2)}) %collective-permute-start) | collective-permute-done | bytes 131104 | tf_op jit(solution)/shard_map/ppermute | solution.py:22
  15.0 1.6 pad_maximum_fusion.1
  16.6 37.2 %all-gather.8.cloned.1.call-done = bf16[8,256,512]{2,1,0:T(8,128)(2,1)} async-done(((bf16[1,256,512]{2,1,0:T(8,128)(2,1)}), bf16[8,256,512]{2,1,0:T(8,128)(2,1)}) %all-gather.8.cloned.1.call-update) | async-done | bytes 2097168 | tf_op jit(solution)/shard_map/all_gather | solution.py:18
  53.9 4.3 %all-to-all-start = ((bf16[8,256,512]{2,1,0:T(8,128)(2,1)}), bf16[8,256,512]{2,1,0:T(8,128)(2,1)S(1)}, u32[]{:S(2)}, u32[]{:S(2)}) async-start(bf16[8,256,512]{2,1,0:T(8,128)(2,1)} %all-gather.8.cloned.1.call-done), calls=%async_computation | async-start | bytes 4194304 | tf_op jit(solution)/shard_map/all_to_all | solution.py:19
  58.2 37.3 %all-gather.6.cloned.1.call-done = bf16[2,256,2048]{2,1,0:T(8,128)(2,1)} async-done(((bf16[2,256,256]{2,1,0:T(8,128)(2,1)}), bf16[2,256,2048]{2,1,0:T(8,128)(2,1)}) %all-gather.6.cloned.1.call-update) | async-done | bytes 2097168 | tf_op jit(solution)/shard_map/all_gather | solution.py:24
  96.8 2.0 convolution_convert_fusion
  98.9 2.2 collective-permute-start.1
  101.0 2.3 fusion.6
  103.4 5.6 %collective-permute-done.1 = bf16[256,512]{1,0:T(8,128)(2,1)S(1)} collective-permute-done((bf16[256,512]{1,0:T(8,128)(2,1)S(1)}, bf16[256,512]{1,0:T(8,128)(2,1)S(1)}, u32[]{:S(2)}, u32[]{:S(2)}) %collective-permute-start.1) | collective-permute-done | bytes 262176 | tf_op jit(solution)/shard_map/ppermute | solution.py:27
  109.3 12.5 %all-reduce = (f32[256]{0:T(256)S(1)}, f32[256]{0:T(256)S(1)}) all-reduce(f32[256]{0:T(256)S(1)} %get-tuple-element.3, f32[256]{0:T(256)S(1)} %get-tuple-element.2), channel_id=1, replica_groups=mesh['section'=2,'z'=8,'xh'=2,'tp'=8] {'tp'}, use_global_device_ids=true, to_apply=%region_3.4 | all-reduce | flops 512 | bytes 4096 | tf_op jit(solution)/shard_map/psum | solution.py:33
  123.1 2.5 collective-permute-start.2
  125.6 11.4 %collective-permute-done.2 = bf16[256,1024]{1,0:T(8,128)(2,1)S(1)} collective-permute-done((bf16[256,1024]{1,0:T(8,128)(2,1)}, bf16[256,1024]{1,0:T(8,128)(2,1)S(1)}, u32[]{:S(2)}, u32[]{:S(2)}) %collective-permute-start.2) | collective-permute-done | bytes 524320 | tf_op jit(solution)/shard_map/ppermute | solution.py:42
  137.3 2.5 collective-permute-start.3
  139.8 6.2 %collective-permute-done.3 = bf16[256,512]{1,0:T(8,128)(2,1)S(1)} collective-permute-done((bf16[256,512]{1,0:T(8,128)(2,1)S(1)}, bf16[256,512]{1,0:T(8,128)(2,1)S(1)}, u32[]{:S(2)}, u32[]{:S(2)}) %collective-permute-start.3) | collective-permute-done | bytes 262176 | tf_op jit(solution)/shard_map/ppermute | solution.py:50
  147.4 33.4 %all-gather.12.cloned.1.call-done = bf16[16,256,512]{2,1,0:T(8,128)(2,1)} async-done(((bf16[2,256,512]{2,1,0:T(8,128)(2,1)}), bf16[16,256,512]{2,1,0:T(8,128)(2,1)}) %all-gather.12.cloned.1.call-update) | async-done | bytes 4194320 | tf_op jit(solution)/shard_map/all_gather | solution.py:51
  180.8 4.5 %copy.11 = bf16[8,2,256,512]{3,0,2,1:T(8,128)(2,1)S(1)} copy(bf16[8,2,256,512]{3,2,1,0:T(8,128)(2,1)} %bitcast.47) | data formatting | bytes 8388608 | tf_op jit(solution)/shard_map/all_gather | solution.py:51
  185.3 4.2 %copy.13 = bf16[64,8,8,512]{3,1,2,0:T(8,128)(2,1)} copy(bf16[64,8,8,512]{3,2,1,0:T(8,128)(2,1)S(1)} %bitcast.45) | data formatting | bytes 8388608
  189.5 87.1 %all-gather.10.cloned.1.call-done = bf16[8,1024,512]{2,1,0:T(8,128)(2,1)} async-done(((bf16[1,1024,512]{2,1,0:T(8,128)(2,1)}), bf16[8,1024,512]{2,1,0:T(8,128)(2,1)}) %all-gather.10.cloned.1.call-update) | async-done | bytes 8388624 | tf_op jit(solution)/shard_map/all_gather | solution.py:20
  276.6 11.5 %copy.12 = bf16[8,1024,512]{1,2,0:T(8,128)(2,1)} copy(bf16[8,1024,512]{2,1,0:T(8,128)(2,1)} %all-gather.10.cloned.1.call-done) | data formatting | bytes 16777216 | tf_op jit(solution)/shard_map/all_gather | solution.py:20
  288.1 8.1 %fusion.10 = f32[512,1024]{1,0:T(8,128)S(1)} fusion(bf16[512,4096]{1,0:T(8,128)(2,1)} %bitcast.48, bf16[1024,4096]{0,1:T(8,128)(2,1)} %bitcast.46), kind=kOutput, calls=%fused_computation.30 | convolution fusion | flops 4294967296 | bytes 14680064 | tf_op jit(solution)/shard_map/dot_general | solution.py:52
  296.3 2.2 collective-permute-start.4
  298.5 1.4 fusion.8
  299.9 11.7 %collective-permute-done.4 = bf16[256,1024]{1,0:T(8,128)(2,1)S(1)} collective-permute-done((bf16[256,1024]{1,0:T(8,128)(2,1)S(1)}, bf16[256,1024]{1,0:T(8,128)(2,1)S(1)}, u32[]{:S(2)}, u32[]{:S(2)}) %collective-permute-start.4) | collective-permute-done | bytes 524320 | tf_op jit(solution)/shard_map/ppermute | solution.py:58
  (30 shorter events, 6.5 us)
Async XLA Ops:
  7.2 46.7 %all-gather.8.cloned.1.call-start = ((), (), s32[]{:S(2)}) async-start(), calls=%async_computation.2 | async-start | bytes 2359296 | tf_op jit(solution)/shard_map/all_gather | solution.py:18
  7.9 87.6 %all-gather.6.cloned.1.call-start = ((), (), s32[]{:S(2)}) async-start(), calls=%async_computation.1 | async-start | bytes 2359296 | tf_op jit(solution)/shard_map/all_gather | solution.py:24
  7.9 7.0 %collective-permute-start = (bf16[256,256]{1,0:T(8,128)(2,1)}, bf16[256,256]{1,0:T(8,128)(2,1)S(1)}, u32[]{:S(2)}, u32[]{:S(2)}) collective-permute-start(bf16[256,256]{1,0:T(8,128)(2,1)} %bitcast.52), channel_id=1, source_target_pairs={{0,8},{8,0},{1,9},{9,1},{2,10},{10,2},{3,11},{11,3},{4,12},{12,4},... | collective-permute-start | bytes 393224 | tf_op jit(solution)/shard_map/ppermute | solution.py:22
  53.9 41.6 %all-to-all-start = ((bf16[8,256,512]{2,1,0:T(8,128)(2,1)}), bf16[8,256,512]{2,1,0:T(8,128)(2,1)S(1)}, u32[]{:S(2)}, u32[]{:S(2)}) async-start(bf16[8,256,512]{2,1,0:T(8,128)(2,1)} %all-gather.8.cloned.1.call-done), calls=%async_computation | async-start | bytes 4194304 | tf_op jit(solution)/shard_map/all_to_all | solution.py:19
  58.2 122.6 %all-gather.12.cloned.1.call-start = ((), (), s32[]{:S(2)}) async-start(), calls=%async_computation.4 | async-start | bytes 4718592 | tf_op jit(solution)/shard_map/all_gather | solution.py:51
  95.5 1.3 copy-start.3
  95.5 5.5 %copy-start.5 = (bf16[2,256,2048]{2,1,0:T(8,128)(2,1)S(1)}, bf16[2,256,2048]{2,1,0:T(8,128)(2,1)}, u32[]{:S(2)}) copy-start(bf16[2,256,2048]{2,1,0:T(8,128)(2,1)} %all-gather.6.cloned.1.call-done) | copy-start | bytes 6291460
  98.8 10.1 %copy-start.2 = (bf16[1,256,1024]{2,1,0:T(8,128)(2,1)S(1)}, bf16[1,256,1024]{2,1,0:T(8,128)(2,1)}, u32[]{:S(2)}) copy-start(bf16[1,256,1024]{2,1,0:T(8,128)(2,1)} %param.7) | copy-start | bytes 1572868
  98.9 10.1 %copy-start.4 = (f32[1,1024]{1,0:T(1,128)S(1)}, f32[1,1024]{1,0:T(1,128)}, u32[]{:S(2)}) copy-start(f32[1,1024]{1,0:T(1,128)} %param.8) | copy-start | bytes 12292
  98.9 10.1 %collective-permute-start.1 = (bf16[256,512]{1,0:T(8,128)(2,1)S(1)}, bf16[256,512]{1,0:T(8,128)(2,1)S(1)}, u32[]{:S(2)}, u32[]{:S(2)}) collective-permute-start(bf16[256,512]{1,0:T(8,128)(2,1)S(1)} %convolution_convert_fusion), channel_id=1, source_target_pairs={{0,8},{8,0},{1,9},{9,1},{2,10},{10,2},{3,11},{11,3},{4,12},{12,4},... | collective-permute-start | bytes 786440 | tf_op jit(solution)/shard_map/ppermute | solution.py:27
  103.3 18.5 %copy-start = (bf16[256,1024]{1,0:T(8,128)(2,1)S(1)}, bf16[256,1024]{1,0:T(8,128)(2,1)}, u32[]{:S(2)}) copy-start(bf16[256,1024]{1,0:T(8,128)(2,1)} %param.12) | copy-start | bytes 1572868
  103.3 18.5 %copy-start.1 = (bf16[1,256,1024]{2,1,0:T(8,128)(2,1)S(1)}, bf16[1,256,1024]{2,1,0:T(8,128)(2,1)}, u32[]{:S(2)}) copy-start(bf16[1,256,1024]{2,1,0:T(8,128)(2,1)} %param.11) | copy-start | bytes 1572868
  123.1 13.9 %collective-permute-start.2 = (bf16[256,1024]{1,0:T(8,128)(2,1)}, bf16[256,1024]{1,0:T(8,128)(2,1)S(1)}, u32[]{:S(2)}, u32[]{:S(2)}) collective-permute-start(bf16[256,1024]{1,0:T(8,128)(2,1)} %add_convert_fusion.1), channel_id=1, source_target_pairs={{128,0},{129,1},{130,2},{131,3},{132,4},{133,5},{134,6},{135,7},{1... | collective-permute-start | bytes 1572872 | tf_op jit(solution)/shard_map/ppermute | solution.py:42
  137.3 8.7 %collective-permute-start.3 = (bf16[256,512]{1,0:T(8,128)(2,1)S(1)}, bf16[256,512]{1,0:T(8,128)(2,1)S(1)}, u32[]{:S(2)}, u32[]{:S(2)}) collective-permute-start(bf16[256,512]{1,0:T(8,128)(2,1)S(1)} %get-tuple-element.7), channel_id=1, source_target_pairs={{0,8},{8,0},{1,9},{9,1},{2,10},{10,2},{3,11},{11,3},{4,12},{12,4},... | collective-permute-start | bytes 786440 | tf_op jit(solution)/shard_map/ppermute | solution.py:50
  146.9 129.7 %all-gather.10.cloned.1.call-start = ((), (), s32[]{:S(2)}) async-start(), calls=%async_computation.3 | async-start | bytes 9437184 | tf_op jit(solution)/shard_map/all_gather | solution.py:20
  296.3 15.3 %collective-permute-start.4 = (bf16[256,1024]{1,0:T(8,128)(2,1)S(1)}, bf16[256,1024]{1,0:T(8,128)(2,1)S(1)}, u32[]{:S(2)}, u32[]{:S(2)}) collective-permute-start(bf16[256,1024]{1,0:T(8,128)(2,1)S(1)} %slice.45), channel_id=1, source_target_pairs={{0,8},{8,0},{1,9},{9,1},{2,10},{10,2},{3,11},{11,3},{4,12},{12,4},... | collective-permute-start | bytes 1572872 | tf_op jit(solution)/shard_map/ppermute | solution.py:58
Sparse Core Ops, SparseCore 0:
  9.8 44.0 all-gather.7
  56.3 39.1 all-gather.5
  147.0 33.7 all-gather.11
  182.4 94.0 all-gather.9

commit v2 on v1

v2 whole, which is shorter than its diff:
```python
import jax
import jax.numpy as jnp
from jax import lax
from jax.experimental import pallas as pl
from jax.experimental.pallas import tpu as pltpu
from jax.sharding import Mesh, PartitionSpec as P

D = 8192
epsilon = 1e-05
SEQ = ("z", "xh")
Z = 8
CHUNKS = 2
F32, BF16 = jnp.float32, jnp.bfloat16


def rcopy(src, dst, send_sem, recv_sem, **to):
    return pltpu.make_async_remote_copy(
        src_ref=src, dst_ref=dst, send_sem=send_sem, recv_sem=recv_sem,
        device_id=to, device_id_type=pl.DeviceIdType.MESH,
    )


def arrived(ref, sem):
    pltpu.make_async_copy(ref, ref, sem).wait()


def kernel(
    li, gain, cot_hbm, kvw_hbm, mlp, oc, wo_hbm, attn_out, ig_out,
    cotb, wz, wk, pair, wo, own_terms, their_terms, tin, give, arr, stat, coef, acc, back, pout, pin,
    kv_s, kv_r, a2a_s, a2a_r, cot_s, cot_r, gr_s, gr_r, st_s, st_r, wo_s, wo_r, one_s, one_r, loc,
):
    s, z = lax.axis_index("section"), lax.axis_index("z")
    h, t = lax.axis_index("xh"), lax.axis_index("tp")
    hp = 1 - h
    y, c = t // 2, t % 2
    zr, zl = (z + 1) % Z, (z + Z - 1) % Z
    yr, yl, yo = [((y + i) % 4) * 2 + c for i in (1, 3, 2)]
    core, yr_c, yl_c, yo_c = [i + 1 - 2 * c for i in (t, yr, yl, yo)]

    barrier = pltpu.get_barrier_semaphore()
    greet = [{"xh": hp}, {"section": 1 - s}, {"z": zr}, {"z": zl}]
    greet += [{"tp": (t + i) % Z} for i in range(1, Z)]
    for to in greet:
        pl.semaphore_signal(barrier, inc=1, device_id=to, device_id_type=pl.DeviceIdType.MESH)
    pl.semaphore_wait(barrier, len(greet))

    sent = []

    def send(src, dst, send_sem, recv_sem, **to):
        copy = rcopy(src, dst, send_sem, recv_sem, **to)
        copy.start()
        sent.append(copy)

    def ring_start(own, slot, ss, rs):
        send(own, slot(z), ss.at[0], rs.at[0], z=zr)
        send(own, slot(z), ss.at[4], rs.at[4], z=zl)

    def ring_step(k, slot, rows, ss, rs):
        a, b = (z + Z - k) % Z, (z + k) % Z
        first, last = pl.ds(0, rows // 2), pl.ds(rows // 2, rows // 2)
        if k < 4:
            arrived(slot(a), rs.at[k - 1])
            part = slot(a) if k < 3 else slot(a).at[first]
            send(part, part, ss.at[k], rs.at[k], z=zr)
            arrived(slot(b), rs.at[k + 3])
            part = slot(b) if k < 3 else slot(b).at[last]
            send(part, part, ss.at[k + 4], rs.at[k + 4], z=zl)
        else:
            arrived(slot(a).at[first], rs.at[3])
            arrived(slot(a).at[last], rs.at[7])

    def swap_start(buf, ss, rs):
        own = buf.at[t]
        send(own, own, ss.at[0], rs.at[0], tp=yr)
        send(own, own, ss.at[1], rs.at[1], tp=yl)
        send(own, own, ss.at[2], rs.at[4], tp=core)

    def swap_near(buf, ss, rs):
        arrived(buf.at[yl], rs.at[0])
        send(buf.at[yl, 0], buf.at[yl, 0], ss.at[3], rs.at[2], tp=yr)
        send(buf.at[yl], buf.at[yl], ss.at[4], rs.at[5], tp=core)
        arrived(buf.at[yr], rs.at[1])
        send(buf.at[yr, 1], buf.at[yr, 1], ss.at[5], rs.at[3], tp=yl)
        send(buf.at[yr], buf.at[yr], ss.at[6], rs.at[6], tp=core)

    def swap_far(buf, ss, rs):
        arrived(buf.at[yo, 0], rs.at[2])
        arrived(buf.at[yo, 1], rs.at[3])
        send(buf.at[yo], buf.at[yo], ss.at[7], rs.at[7], tp=core)

    def swap_end(buf, rs):
        for index, place in enumerate((core, yl_c, yr_c, yo_c)):
            arrived(buf.at[place], rs.at[4 + index])

    def pass_on(block, zz):
        @pl.when(zz == t)
        def _():
            pltpu.make_async_copy(block, wk.at[t], a2a_r.at[t]).start()

        @pl.when(zz != t)
        def _():
            rcopy(block, wk.at[t], a2a_s.at[zz], a2a_r.at[t], tp=zz).start()

    kv_slot = lambda i: wz.at[i]
    chunk_rows = 1024 // CHUNKS
    wo_slot = lambda j: (lambda i: wo.at[i, pl.ds(j * chunk_rows, chunk_rows)])

    def kv_step(k):
        ring_step(k, kv_slot, 256, kv_s, kv_r)
        if k < 4:
            pass_on(wz.at[(z + Z - k) % Z], (z + Z - k) % Z)
            pass_on(wz.at[(z + k) % Z], (z + k) % Z)
        else:
            pass_on(wz.at[(z + 4) % Z], (z + 4) % Z)

    def wo_step(k):
        for j in range(CHUNKS):
            ring_step(k, wo_slot(j), chunk_rows, wo_s.at[j], wo_r.at[j])

    ring_start(kvw_hbm, kv_slot, kv_s, kv_r)
    send(cot_hbm, cotb.at[t, h], one_s.at[0], one_r.at[0], xh=hp)
    cot_own = pltpu.make_async_copy(cot_hbm, cotb.at[t, h], loc.at[0])
    cot_own.start()
    wo_own = pltpu.make_async_copy(wo_hbm, wo.at[z], loc.at[1])
    wo_own.start()
    pass_on(kvw_hbm, z)

    @pl.loop(0, 8)
    def _(i):
        rows = pl.ds(pl.multiple_of(i * 32, 32), 32)
        v = li[rows, :].astype(F32)
        coef[rows, :] = jnp.broadcast_to(jnp.sum(v * v, axis=1, keepdims=True), (32, 128))

    cot_own.wait()
    arrived(cotb.at[t, hp], one_r.at[0])
    swap_start(cotb, cot_s, cot_r)
    kv_step(1)
    for j in range(CHUNKS):
        ring_start(wo_hbm.at[pl.ds(j * chunk_rows, chunk_rows)], wo_slot(j), wo_s.at[j], wo_r.at[j])
    swap_near(cotb, cot_s, cot_r)
    kv_step(2)
    swap_far(cotb, cot_s, cot_r)
    kv_step(3)
    kv_step(4)
    swap_end(cotb, cot_r)
    for i in range(Z):
        arrived(wk.at[i], a2a_r.at[i])

    def terms(half, into):
        into[...] = jnp.dot(cotb[0, half], wk[0], preferred_element_type=F32)

        @pl.loop(1, Z)
        def _(i):
            into[...] += jnp.dot(cotb[i, half], wk[i], preferred_element_type=F32)

    terms(hp, own_terms)
    their_terms[...] = own_terms[...].astype(BF16)
    send(their_terms, tin, one_s.at[1], one_r.at[1], xh=hp)
    terms(h, own_terms)

    mine = pl.ds(pl.multiple_of(h * 512, 512), 512)
    other = pl.ds(pl.multiple_of(hp * 512, 512), 512)
    lane = lax.broadcasted_iota(jnp.int32, (32, 128), 1)
    arrived(tin, one_r.at[1])

    @pl.loop(0, 8)
    def _(i):
        rows = pl.ds(pl.multiple_of(i * 32, 32), 32)
        inner = jnp.sum(gain[:, mine] * own_terms[rows, :] * li[rows, mine].astype(F32), axis=1, keepdims=True)
        inner += jnp.sum(
            gain[:, other] * tin[rows, :].astype(F32) * li[rows, other].astype(F32), axis=1, keepdims=True
        )
        coef[rows, :] = jnp.where(lane == 0, coef[rows, :], jnp.broadcast_to(inner, (32, 128)))

    stat[t] = coef[...].T[:8]
    for i in range(1, Z):
        send(stat.at[t], stat.at[t], st_s.at[i], st_r.at[t], tp=(t + i) % Z)
    for i in range(1, Z):
        place = (t + i) % Z
        arrived(stat.at[place], st_r.at[place])
    total = stat[0]
    for i in range(1, Z):
        total += stat[i]
    inv = lax.rsqrt(total / D + epsilon)
    inv = jnp.broadcast_to(inv[0:1], (8, 256))
    both = jnp.where(
        lax.broadcasted_iota(jnp.int32, (8, 256), 0) == 0, inv, inv * inv * inv * total / D
    )
    coef[...] = jnp.concatenate([both] * 16, axis=0).T

    @pl.loop(0, 8)
    def _(i):
        rows = pl.ds(pl.multiple_of(i * 32, 32), 32)
        scale, shift = coef[rows, 0:1], coef[rows, 1:2]
        back[rows, mine] = scale * gain[:, mine] * own_terms[rows, :] - li[rows, mine].astype(F32) * shift
        back[rows, other] = (
            scale * gain[:, other] * tin[rows, :].astype(F32) - li[rows, other].astype(F32) * shift
        )

    onward = rcopy(ig_out, arr, one_s.at[2], one_r.at[2], section=1 - s)

    @pl.when(s == 1)
    def _():
        @pl.loop(0, 8)
        def _(i):
            rows = pl.ds(pl.multiple_of(i * 32, 32), 32)
            grad = oc[rows, :].astype(F32) + mlp[rows, :].astype(F32)
            ig_out[rows, :] = (grad + back[rows, :]).astype(BF16)

        onward.start()

    wo_step(1)

    def cast(first):
        @pl.loop(0, 8)
        def _(i):
            rows = pl.ds(pl.multiple_of(i * 32, 32), 32)
            pair[t, h, rows, :] = (first[rows, mine].astype(F32) + mlp[rows, mine].astype(F32)).astype(BF16)
            give[rows, :] = (first[rows, other].astype(F32) + mlp[rows, other].astype(F32)).astype(BF16)

    @pl.when(s == 1)
    def _():
        cast(oc)

    @pl.when(s == 0)
    def _():
        arrived(arr, one_r.at[2])
        cast(arr)

    send(give, pair.at[t, h], one_s.at[3], one_r.at[3], xh=hp)

    @pl.when(s == 0)
    def _():
        @pl.loop(0, 8)
        def _(i):
            rows = pl.ds(pl.multiple_of(i * 32, 32), 32)
            grad = arr[rows, :].astype(F32) + mlp[rows, :].astype(F32)
            ig_out[rows, :] = (grad + back[rows, :]).astype(BF16)

    arrived(pair.at[t, hp], one_r.at[3])
    swap_start(pair, gr_s, gr_r)
    wo_step(2)
    swap_near(pair, gr_s, gr_r)
    swap_far(pair, gr_s, gr_r)
    wo_step(3)
    swap_end(pair, gr_r)
    wo_own.wait()

    def block(i, first=False):
        @pl.loop(0, 4)
        def _(n):
            columns = pl.ds(pl.multiple_of(n * 256, 256), 256)
            product = lax.dot_general(
                pair[i].reshape(512, 512), wo[i, columns, :],
                (((1,), (1,)), ((), ())), preferred_element_type=F32,
            )
            if first:
                acc[:, columns] = product
            else:
                acc[:, columns] += product

    block(z, True)
    for k in (1, 2, 3):
        block((z + Z - k) % Z)
        block((z + k) % Z)
    wo_step(4)
    block((z + 4) % Z)
    theirs = pl.ds(pl.multiple_of(hp * 256, 256), 256)
    ours = pl.ds(pl.multiple_of(h * 256, 256), 256)
    pout[...] = acc[theirs, :].astype(BF16)
    send(pout, pin, one_s.at[4], one_r.at[4], xh=hp)
    arrived(pin, one_r.at[4])
    attn_out[...] = (acc[ours, :] + pin[...].astype(F32)).astype(BF16)

    for copy in sent:
        copy.wait_send()
    for i in range(Z):
        @pl.when(i != t)
        def _():
            rcopy(wk.at[t], wk.at[t], a2a_s.at[i], a2a_r.at[t], tp=i).wait_send()

    @pl.when(s == 1)
    def _():
        onward.wait_send()


def body(layer_input, norm_gain, kv_cotangent, kv_weight, mlp_grads, output_cotangent, out_weight):
    vmem, hbm = pl.BlockSpec(memory_space=pltpu.VMEM), pl.BlockSpec(memory_space=pl.ANY)
    dma = lambda *n: pltpu.SemaphoreType.DMA(n)
    out = jax.ShapeDtypeStruct((256, 1024), BF16)
    attn, grads = pl.pallas_call(
        kernel,
        out_shape=(out, out),
        in_specs=[vmem, vmem, hbm, hbm, vmem, vmem, hbm],
        out_specs=(vmem, vmem),
        scratch_shapes=[
            pltpu.VMEM((Z, 2, 256, 256), BF16),
            pltpu.VMEM((Z, 256, 512), BF16),
            pltpu.VMEM((Z, 256, 512), BF16),
            pltpu.VMEM((Z, 2, 256, 512), BF16),
            pltpu.VMEM((Z, 1024, 512), BF16),
            pltpu.VMEM((256, 512), F32),
            pltpu.VMEM((256, 512), BF16),
            pltpu.VMEM((256, 512), BF16),
            pltpu.VMEM((256, 512), BF16),
            pltpu.VMEM((256, 1024), BF16),
            pltpu.VMEM((Z, 8, 256), F32),
            pltpu.VMEM((256, 128), F32),
            pltpu.VMEM((512, 1024), F32),
            pltpu.VMEM((256, 1024), F32),
            pltpu.VMEM((256, 1024), BF16),
            pltpu.VMEM((256, 1024), BF16),
            dma(8), dma(8),
            dma(8), dma(8),
            dma(8), dma(8),
            dma(8), dma(8),
            dma(8), dma(8),
            dma(CHUNKS, 8), dma(CHUNKS, 8),
            dma(5), dma(5),
            dma(2),
        ],
        compiler_params=pltpu.CompilerParams(
            collective_id=0, has_side_effects=True, vmem_limit_bytes=48 * 2**20
        ),
    )(
        layer_input[0], norm_gain, kv_cotangent[0], kv_weight[0],
        mlp_grads[0], output_cotangent, out_weight[0],
    )
    return attn[None], grads[None]


def solution(mesh):
    fine = Mesh(
        mesh.devices.reshape(mesh.shape["section"], Z, 2, mesh.shape["tp"]),
        ("section", "z", "xh", "tp"),
    )
    in_specs = (
        P("section", SEQ, "tp"),
        P("section", "tp"),
        P("section", SEQ, "tp"),
        P("section", "tp", SEQ),
        P("section", SEQ, "tp"),
        P(SEQ, "tp"),
        P("section", "tp", SEQ),
    )
    out_specs = (P("section", SEQ, "tp"), P("section", SEQ, "tp"))
    return jax.shard_map(body, mesh=fine, in_specs=in_specs, out_specs=out_specs, check_vma=False)
```

time: 320 us -> 171 us (0.53)
  waiting for transfers between devices: 236 us -> 0 us
  Pallas kernels: 0 us -> 161 us
  starting transfers between devices: 16 us -> 0 us
  between operations: 13.9 us -> 0.66 us
  local copies, waits for them, and re-layouts: 21.6 us -> 8.47 us
  blocking collectives: 12.5 us -> 0 us
  matrix products: 12.4 us -> 0 us
  other arithmetic: 6.78 us -> 0 us
    all_gather x4 -> x0, waiting for transfers between devices: 195 us -> none  [the longest x1 87.1 us: body(): out_w = lax.all_gather(out_weight[0], 'z', axis=0)]
    pallas_call x0 -> x1, Pallas kernels: none -> 161 us  [body(): pl.pallas_call(kernel, out_shape=(out, out), in_specs=[vmem, vmem, hbm, h...]
    ppermute x5 -> x0, waiting for transfers between devices: 39.7 us -> none  [the longest x1 11.7 us: body(): other = lax.ppermute(parts[256:].astype(jnp.bfloat16), 'xh', swap)]
    all_gather x2 -> x0, local copies, waits for them, and re-layouts: 16 us -> none  [the longest x1 11.5 us: body(): out_w = lax.all_gather(out_weight[0], 'z', axis=0)]
    psum x1 -> x0, blocking collectives: 12.5 us -> none  [body(): lax.psum((squares, jnp.sum(gain * kv_share * values, axis=1)), 'tp')]
    dot_general x3 -> x0, matrix products: 12.4 us -> none  [the longest x1 8.14 us: body(): lax.dot_general(pair.transpose(1, 2, 0, 3).reshape(512, 4096), out_w.tran...]
    ppermute x5 -> x0, starting transfers between devices: 11.5 us -> none  [the longest x1 2.49 us: body(): arriving = lax.ppermute(input_one, 'section', [(1, 0)])]
    all_to_all x1 -> x0, starting transfers between devices: 4.29 us -> none  [body(): kvw = lax.all_to_all(kvw, 'tp', 0, 0, tiled=True).reshape(2048, 512)]
  transfers between devices with their start and end apart: 10 -> 0, of which waited for: 9 -> 0; matrix products, arithmetic and copies ran while one was open for 4% -> 0% of each run, Pallas kernels for 0% -> 0%
where the time goes in v2:
time: 171 us; the launch traced here: 170 us
  Pallas kernels  161 us (94%)
  local copies, waits for them, and re-layouts  8.47 us (5%)
    pallas_call x1, Pallas kernels, body(): pl.pallas_call(kernel, out_shape=(out, out), in_specs=[vmem, vmem, hbm, h...  161 us
    unnamed x16, local copies, waits for them, and re-layouts  8.47 us

profile of v2, /device:TPU:2, one launch (start us, length us, event | category | flops | bytes accessed | tf_op | source)
XLA Modules:
  0.0 170.0 jit_solution(3015614268577413451)
XLA Ops:
  0.6 0.0 copy-start.6
  0.6 0.7 copy-done.6
  1.3 0.0 copy-start
  1.3 1.2 copy-done
  2.5 0.0 copy-start.1
  2.5 1.0 copy-done.1
  3.6 0.0 copy-start.2
  3.6 1.0 copy-done.2
  4.6 0.0 copy-start.3
  4.6 1.0 copy-done.3
  5.7 0.0 copy-start.4
  5.7 0.9 copy-done.4
  6.6 0.0 copy-start.5
  6.6 0.9 copy-done.5
  7.5 160.8 %shard_map.86 = (bf16[256,1024]{1,0:T(8,128)(2,1)S(1)}, bf16[256,1024]{1,0:T(8,128)(2,1)S(1)}) custom-call(bf16[256,1024]{1,0:T(8,128)(2,1)S(1)} %bitcast.10, f32[1,1024]{1,0:T(1,128)S(1)} %copy-done.6, bf16[256,256]{1,0:T(8,128)(2,1)S(1)} %bitcast.13, bf16[256,512]{1,0:T(8,128)(2,1)S(1)} %bitcast.12, bf16[256,1024]{1,0:T(8,128)(2,1)S(1)} %bitcast.11, ...), custom_call_target="tpu_custom_call" | custom-call | tf_op jit(solution)/shard_map/pallas_call | solution.py:291
  168.4 0.8 copy.11
  169.2 0.8 copy.12
Async XLA Ops:
  0.6 0.7 copy-start.6
  1.3 1.2 copy-start
  2.5 1.0 copy-start.1
  3.6 1.0 copy-start.2
  4.6 1.0 copy-start.3
  5.7 0.9 copy-start.4
  6.6 0.9 copy-start.5

commit v3 on v2

v3 whole, which is shorter than its diff:
```python
import jax
import jax.numpy as jnp
from jax import lax
from jax.experimental import pallas as pl
from jax.experimental.pallas import tpu as pltpu
from jax.sharding import Mesh, PartitionSpec as P

D = 8192
epsilon = 1e-05
SEQ = ("z", "xh")
Z = 8
CHUNKS = 4
KV_CHUNKS = 4
F32, BF16 = jnp.float32, jnp.bfloat16


def rcopy(src, dst, send_sem, recv_sem, **to):
    return pltpu.make_async_remote_copy(
        src_ref=src, dst_ref=dst, send_sem=send_sem, recv_sem=recv_sem,
        device_id=to, device_id_type=pl.DeviceIdType.MESH,
    )


def arrived(ref, sem):
    pltpu.make_async_copy(ref, ref, sem).wait()


def kernel(
    li_hbm, gain_hbm, cot_hbm, kvw_hbm, mlp_hbm, oc_hbm, wo_hbm, attn_out, ig_out,
    li, gain, mlp, oc, cotb, wz, wk, pair, wo, own_terms, their_terms, tin, give,
    far_in, keep_in, rest_in, stat, coef, acc, pout, pin,
    kv_s, kv_r, a2a_s, a2a_r, cot_s, cot_r, gr_s, gr_r, st_s, st_r, wo_s, wo_r, one_s, one_r, out_s, out_r, loc,
):
    s, z = lax.axis_index("section"), lax.axis_index("z")
    h, t = lax.axis_index("xh"), lax.axis_index("tp")
    hp = 1 - h
    y, c = t // 2, t % 2
    zr, zl = (z + 1) % Z, (z + Z - 1) % Z
    yr, yl, yo = [((y + i) % 4) * 2 + c for i in (1, 3, 2)]
    core, yr_c, yl_c, yo_c = [i + 1 - 2 * c for i in (t, yr, yl, yo)]
    mine = pl.ds(pl.multiple_of(h * 512, 512), 512)
    other = pl.ds(pl.multiple_of(hp * 512, 512), 512)

    loads = [
        pltpu.make_async_copy(src, dst, loc.at[i])
        for i, (src, dst) in enumerate(((li_hbm, li), (gain_hbm, gain), (mlp_hbm, mlp), (oc_hbm, oc)))
    ]
    cot_own = pltpu.make_async_copy(cot_hbm, cotb.at[t, h], loc.at[4])
    wo_own = pltpu.make_async_copy(wo_hbm, wo.at[z], loc.at[5])
    for load in [cot_own] + loads + [wo_own]:
        load.start()

    barrier = pltpu.get_barrier_semaphore()
    greet = [{"xh": hp}, {"section": 1 - s}, {"section": 1 - s, "xh": hp}, {"z": zr}, {"z": zl}]
    greet += [{"tp": (t + i) % Z} for i in range(1, Z)]
    for to in greet:
        pl.semaphore_signal(barrier, inc=1, device_id=to, device_id_type=pl.DeviceIdType.MESH)
    pl.semaphore_wait(barrier, len(greet))

    sent = []

    def send(src, dst, send_sem, recv_sem, **to):
        copy = rcopy(src, dst, send_sem, recv_sem, **to)
        copy.start()
        sent.append(copy.wait_send)

    def finish():
        for wait in sent:
            wait()

    def ring_start(own, slot, ss, rs):
        send(own, slot(z), ss.at[0], rs.at[0], z=zr)
        send(own, slot(z), ss.at[4], rs.at[4], z=zl)

    def ring_step(k, slot, rows, ss, rs):
        a, b = (z + Z - k) % Z, (z + k) % Z
        first, last = pl.ds(0, rows // 2), pl.ds(rows // 2, rows // 2)
        if k < 4:
            arrived(slot(a), rs.at[k - 1])
            part = slot(a) if k < 3 else slot(a).at[first]
            send(part, part, ss.at[k], rs.at[k], z=zr)
            arrived(slot(b), rs.at[k + 3])
            part = slot(b) if k < 3 else slot(b).at[last]
            send(part, part, ss.at[k + 4], rs.at[k + 4], z=zl)
        else:
            arrived(slot(a).at[first], rs.at[3])
            arrived(slot(a).at[last], rs.at[7])

    def swap_start(whole, ss, rs):
        own = whole(t)
        send(own, own, ss.at[0], rs.at[0], tp=yr)
        send(own, own, ss.at[1], rs.at[1], tp=yl)
        send(own, own, ss.at[2], rs.at[4], tp=core)

    def swap_near(whole, lower, upper, ss, rs):
        arrived(whole(yl), rs.at[0])
        send(lower(yl), lower(yl), ss.at[3], rs.at[2], tp=yr)
        send(whole(yl), whole(yl), ss.at[4], rs.at[5], tp=core)
        arrived(whole(yr), rs.at[1])
        send(upper(yr), upper(yr), ss.at[5], rs.at[3], tp=yl)
        send(whole(yr), whole(yr), ss.at[6], rs.at[6], tp=core)

    def swap_far(whole, lower, upper, ss, rs):
        arrived(lower(yo), rs.at[2])
        arrived(upper(yo), rs.at[3])
        send(whole(yo), whole(yo), ss.at[7], rs.at[7], tp=core)

    def swap_end(whole, rs):
        for index, place in enumerate((core, yl_c, yr_c, yo_c)):
            arrived(whole(place), rs.at[4 + index])

    kv_rows = 256 // KV_CHUNKS
    kv_part = [pl.ds(j * kv_rows, kv_rows) for j in range(KV_CHUNKS)]

    def kv_start(j):
        ring_start(kvw_hbm.at[kv_part[j]], lambda i: wz.at[i, kv_part[j]], kv_s.at[j], kv_r.at[j])

    def kv_step(k, j):
        ring_step(k, lambda i: wz.at[i, kv_part[j]], kv_rows, kv_s.at[j], kv_r.at[j])

    def pass_on(j):
        land = wk.at[t, kv_part[j]]
        for i in range(1, Z):
            zz = (t + i) % Z
            pl.when(zz != z)(
                rcopy(wz.at[zz, kv_part[j]], land, a2a_s.at[j, i], a2a_r.at[j, t], tp=zz).start
            )
            pl.when(zz == z)(
                rcopy(kvw_hbm.at[kv_part[j]], land, a2a_s.at[j, i], a2a_r.at[j, t], tp=zz).start
            )
            sent.append(rcopy(wz.at[zz, kv_part[j]], land, a2a_s.at[j, i], a2a_r.at[j, t], tp=zz).wait_send)
        pl.when(t != z)(pltpu.make_async_copy(wz.at[t, kv_part[j]], land, a2a_r.at[j, t]).start)
        pl.when(t == z)(pltpu.make_async_copy(kvw_hbm.at[kv_part[j]], land, a2a_r.at[j, t]).start)

    wo_rows = 1024 // CHUNKS
    wo_part = [pl.ds(j * wo_rows, wo_rows) for j in range(CHUNKS)]

    def wo_step(k, j):
        ring_step(k, lambda i: wo.at[i, wo_part[j]], wo_rows, wo_s.at[j], wo_r.at[j])

    cot_whole, cot_lower, cot_upper = lambda i: cotb.at[i], lambda i: cotb.at[i, 0], lambda i: cotb.at[i, 1]

    half_kv = KV_CHUNKS // 2
    group_a, group_b = range(half_kv), range(half_kv, KV_CHUNKS)
    for j in group_a:
        kv_start(j)
    send(cot_hbm, cotb.at[t, h], one_s.at[0], one_r.at[0], xh=hp)
    for load in loads:
        load.wait()

    @pl.when(s == 1)
    def _():
        @pl.loop(0, 8)
        def _(i):
            rows = pl.ds(pl.multiple_of(i * 32, 32), 32)
            pair[t, h, rows, :] = (oc[rows, mine].astype(F32) + mlp[rows, mine].astype(F32)).astype(BF16)
            give[rows, :] = (oc[rows, other].astype(F32) + mlp[rows, other].astype(F32)).astype(BF16)

    @pl.when(s == 0)
    def _():
        give[...] = mlp[:, other]

    send(give, pair.at[t, h], one_s.at[3], one_r.at[3], xh=hp)
    cot_own.wait()
    arrived(cotb.at[t, hp], one_r.at[0])
    swap_start(cot_whole, cot_s, cot_r)
    for k in (1, 2):
        for j in group_a:
            kv_step(k, j)
    for j in group_b:
        kv_start(j)
    for j in group_a:
        kv_step(3, j)

    @pl.loop(0, 8)
    def _(i):
        rows = pl.ds(pl.multiple_of(i * 32, 32), 32)
        v = li[rows, :].astype(F32)
        coef[rows, :] = jnp.broadcast_to(jnp.sum(v * v, axis=1, keepdims=True), (32, 128))

    swap_near(cot_whole, cot_lower, cot_upper, cot_s, cot_r)
    for j in group_a:
        kv_step(4, j)
        pass_on(j)
    for j in group_b:
        kv_step(1, j)
    swap_far(cot_whole, cot_lower, cot_upper, cot_s, cot_r)
    for k in (2, 3):
        for j in group_b:
            kv_step(k, j)
    for j in range(CHUNKS):
        ring_start(wo_hbm.at[wo_part[j]], lambda i: wo.at[i, wo_part[j]], wo_s.at[j], wo_r.at[j])
    for j in group_b:
        kv_step(4, j)
        pass_on(j)
    swap_end(cot_whole, cot_r)
    for j in range(KV_CHUNKS):
        for i in range(Z):
            arrived(wk.at[i, kv_part[j]], a2a_r.at[j, i])

    def terms(half, into):
        into[...] = jnp.dot(cotb[0, half], wk[0], preferred_element_type=F32)

        @pl.loop(1, Z)
        def _(i):
            into[...] += jnp.dot(cotb[i, half], wk[i], preferred_element_type=F32)

    terms(hp, own_terms)
    their_terms[...] = own_terms[...].astype(BF16)
    send(their_terms, tin, one_s.at[1], one_r.at[1], xh=hp)
    wo_step(1, 0)
    terms(h, own_terms)
    lane = lax.broadcasted_iota(jnp.int32, (32, 128), 1)
    wo_step(1, 1)
    arrived(tin, one_r.at[1])

    @pl.loop(0, 8)
    def _(i):
        rows = pl.ds(pl.multiple_of(i * 32, 32), 32)
        inner = jnp.sum(gain[:, mine] * own_terms[rows, :] * li[rows, mine].astype(F32), axis=1, keepdims=True)
        inner += jnp.sum(
            gain[:, other] * tin[rows, :].astype(F32) * li[rows, other].astype(F32), axis=1, keepdims=True
        )
        coef[rows, :] = jnp.where(lane == 0, coef[rows, :], jnp.broadcast_to(inner, (32, 128)))

    stat[t] = coef[...].T[:8]
    for i in range(1, Z):
        send(stat.at[t], stat.at[t], st_s.at[i], st_r.at[t], tp=(t + i) % Z)
    wo_step(1, 2)
    for i in range(1, Z):
        place = (t + i) % Z
        arrived(stat.at[place], st_r.at[place])
    total = stat[0]
    for i in range(1, Z):
        total += stat[i]
    inv = lax.rsqrt(total / D + epsilon)
    inv = jnp.broadcast_to(inv[0:1], (8, 256))
    both = jnp.where(
        lax.broadcasted_iota(jnp.int32, (8, 256), 0) == 0, inv, inv * inv * inv * total / D
    )
    coef[...] = jnp.concatenate([both] * 16, axis=0).T

    def norm_back(rows, columns, terms_ref):
        return (
            coef[rows, 0:1] * gain[:, columns] * terms_ref[rows, :].astype(F32)
            - li[rows, columns].astype(F32) * coef[rows, 1:2]
        )

    to_far = rcopy(ig_out.at[:, other], far_in, one_s.at[2], one_r.at[2], section=1 - s, xh=hp)
    to_keep = rcopy(ig_out.at[:, mine], keep_in, one_s.at[4], one_r.at[4], section=1 - s)
    to_rest = rcopy(ig_out.at[:, other], rest_in, one_s.at[5], one_r.at[5], section=1 - s)
    for copy in (to_far, to_keep, to_rest):
        sent.append(lambda copy=copy: pl.when(s == 1)(copy.wait_send))

    @pl.when(s == 1)
    def _():
        def down(columns, terms_ref):
            @pl.loop(0, 8)
            def _(i):
                rows = pl.ds(pl.multiple_of(i * 32, 32), 32)
                grad = oc[rows, columns].astype(F32) + mlp[rows, columns].astype(F32)
                ig_out[rows, columns] = (grad + norm_back(rows, columns, terms_ref)).astype(BF16)

        down(other, tin)
        to_far.start()
        down(mine, own_terms)
        to_keep.start()
        to_rest.start()

    wo_step(1, 3)
    arrived(pair.at[t, hp], one_r.at[3])

    def pair_refs(half):
        return (
            lambda i: pair.at[i, half], lambda i: pair.at[i, half, pl.ds(0, 128)],
            lambda i: pair.at[i, half, pl.ds(128, 128)],
        )

    theirs, ours = pair_refs(hp), pair_refs(h)

    @pl.when(s == 0)
    def _():
        arrived(far_in, one_r.at[2])

        @pl.loop(0, 8)
        def _(i):
            rows = pl.ds(pl.multiple_of(i * 32, 32), 32)
            pair[t, hp, rows, :] = (far_in[rows, :].astype(F32) + pair[t, hp, rows, :].astype(F32)).astype(BF16)

    swap_start(theirs[0], gr_s.at[0], gr_r.at[0])

    @pl.when(s == 0)
    def _():
        arrived(keep_in, one_r.at[4])

        @pl.loop(0, 8)
        def _(i):
            rows = pl.ds(pl.multiple_of(i * 32, 32), 32)
            pair[t, h, rows, :] = (keep_in[rows, :].astype(F32) + mlp[rows, mine].astype(F32)).astype(BF16)

    swap_start(ours[0], gr_s.at[1], gr_r.at[1])

    wo_step(2, 0)
    wo_step(2, 1)
    swap_near(*theirs, gr_s.at[0], gr_r.at[0])
    wo_step(2, 2)

    @pl.when(s == 0)
    def _():
        arrived(rest_in, one_r.at[5])

        def up(columns, terms_ref, from_ref):
            @pl.loop(0, 8)
            def _(i):
                rows = pl.ds(pl.multiple_of(i * 32, 32), 32)
                grad = from_ref[rows, :].astype(F32) + mlp[rows, columns].astype(F32)
                ig_out[rows, columns] = (grad + norm_back(rows, columns, terms_ref)).astype(BF16)

        up(mine, own_terms, keep_in)
        up(other, tin, rest_in)

    swap_near(*ours, gr_s.at[1], gr_r.at[1])
    swap_far(*theirs, gr_s.at[0], gr_r.at[0])
    wo_step(2, 3)
    swap_far(*ours, gr_s.at[1], gr_r.at[1])
    swap_end(theirs[0], gr_r.at[0])
    wo_own.wait()
    wo_step(3, 0)

    def product(half, i, columns):
        return lax.dot_general(
            pair[i, half], wo[i, columns, :], (((1,), (1,)), ((), ())), preferred_element_type=F32
        )

    near = [z] + [(z + k) % Z for k in (Z - 1, 1, Z - 2, 2)]

    def first_blocks(half):
        @pl.loop(0, 4)
        def _(n):
            columns = pl.ds(pl.multiple_of(n * 256, 256), 256)
            total = product(half, near[0], columns)
            for i in near[1:]:
                total += product(half, i, columns)
            acc[half, :, columns] = total

    first_blocks(hp)
    wo_step(3, 1)
    swap_end(ours[0], gr_r.at[1])
    first_blocks(h)
    for j in range(CHUNKS):
        if j > 1:
            wo_step(3, j)
        for half in (hp, h):
            acc[half, :, wo_part[j]] += product(half, (z + 3) % Z, wo_part[j]) + product(
                half, (z + Z - 3) % Z, wo_part[j]
            )
    for j in range(CHUNKS):
        wo_step(4, j)
        far = (z + 4) % Z
        pout[j] = (acc[hp, :, wo_part[j]] + product(hp, far, wo_part[j])).astype(BF16)
        send(pout.at[j], pin.at[j], out_s.at[j], out_r.at[j], xh=hp)
        acc[h, :, wo_part[j]] += product(h, far, wo_part[j])
    for j in range(CHUNKS):
        arrived(pin.at[j], out_r.at[j])
        attn_out[:, wo_part[j]] = (acc[h, :, wo_part[j]] + pin[j].astype(F32)).astype(BF16)
    finish()


def body(layer_input, norm_gain, kv_cotangent, kv_weight, mlp_grads, output_cotangent, out_weight):
    vmem, hbm = pl.BlockSpec(memory_space=pltpu.VMEM), pl.BlockSpec(memory_space=pltpu.HBM)
    dma = lambda *n: pltpu.SemaphoreType.DMA(n)
    out = jax.ShapeDtypeStruct((256, 1024), BF16)
    attn, grads = pl.pallas_call(
        kernel,
        out_shape=(out, out),
        in_specs=[hbm] * 7,
        out_specs=(vmem, vmem),
        scratch_shapes=[
            pltpu.VMEM((256, 1024), BF16),
            pltpu.VMEM((1, 1024), F32),
            pltpu.VMEM((256, 1024), BF16),
            pltpu.VMEM((256, 1024), BF16),
            pltpu.VMEM((Z, 2, 256, 256), BF16),
            pltpu.VMEM((Z, 256, 512), BF16),
            pltpu.VMEM((Z, 256, 512), BF16),
            pltpu.VMEM((Z, 2, 256, 512), BF16),
            pltpu.VMEM((Z, 1024, 512), BF16),
            pltpu.VMEM((256, 512), F32),
            pltpu.VMEM((256, 512), BF16),
            pltpu.VMEM((256, 512), BF16),
            pltpu.VMEM((256, 512), BF16),
            pltpu.VMEM((256, 512), BF16),
            pltpu.VMEM((256, 512), BF16),
            pltpu.VMEM((256, 512), BF16),
            pltpu.VMEM((Z, 8, 256), F32),
            pltpu.VMEM((256, 128), F32),
            pltpu.VMEM((2, 256, 1024), F32),
            pltpu.VMEM((CHUNKS, 256, 1024 // CHUNKS), BF16),
            pltpu.VMEM((CHUNKS, 256, 1024 // CHUNKS), BF16),
            dma(KV_CHUNKS, 8), dma(KV_CHUNKS, 8),
            dma(KV_CHUNKS, 8), dma(KV_CHUNKS, 8),
            dma(8), dma(8),
            dma(2, 8), dma(2, 8),
            dma(8), dma(8),
            dma(CHUNKS, 8), dma(CHUNKS, 8),
            dma(6), dma(6),
            dma(CHUNKS), dma(CHUNKS),
            dma(6),
        ],
        compiler_params=pltpu.CompilerParams(
            collective_id=0, has_side_effects=True, vmem_limit_bytes=58 * 2**20
        ),
    )(
        layer_input[0], norm_gain, kv_cotangent[0], kv_weight[0],
        mlp_grads[0], output_cotangent, out_weight[0],
    )
    return attn[None], grads[None]


def solution(mesh):
    fine = Mesh(
        mesh.devices.reshape(mesh.shape["section"], Z, 2, mesh.shape["tp"]),
        ("section", "z", "xh", "tp"),
    )
    in_specs = (
        P("section", SEQ, "tp"),
        P("section", "tp"),
        P("section", SEQ, "tp"),
        P("section", "tp", SEQ),
        P("section", SEQ, "tp"),
        P(SEQ, "tp"),
        P("section", "tp", SEQ),
    )
    out_specs = (P("section", SEQ, "tp"), P("section", SEQ, "tp"))
    return jax.shard_map(body, mesh=fine, in_specs=in_specs, out_specs=out_specs, check_vma=False)
```

time: 171 us -> 128 us (0.75)
  Pallas kernels: 161 us -> 125 us
  local copies, waits for them, and re-layouts: 8.47 us -> 2.72 us
    pallas_call x1, Pallas kernels: 161 us -> 125 us  [body(): pl.pallas_call(kernel, out_shape=(out, out), in_specs=[hbm] * 7, out_spec...]
    unnamed x16 -> x4, local copies, waits for them, and re-layouts: 8.47 us -> 2.72 us
where the time goes in v3:
time: 128 us
  Pallas kernels  125 us (98%)
  local copies, waits for them, and re-layouts  2.72 us (2%)
    pallas_call x1, Pallas kernels, body(): pl.pallas_call(kernel, out_shape=(out, out), in_specs=[hbm] * 7, out_spec...  125 us
    unnamed x4, local copies, waits for them, and re-layouts  2.72 us

profile of v3, /device:TPU:2, one launch (start us, length us, event | category | flops | bytes accessed | tf_op | source)
XLA Modules:
  0.0 127.9 jit_solution(11397870685555732206)
XLA Ops:
  0.6 124.5 %shard_map.86 = (bf16[256,1024]{1,0:T(8,128)(2,1)}, bf16[256,1024]{1,0:T(8,128)(2,1)}) custom-call(bf16[256,1024]{1,0:T(8,128)(2,1)} %bitcast.10, f32[1,1024]{1,0:T(1,128)} %gain_hbm.1, bf16[256,256]{1,0:T(8,128)(2,1)} %bitcast.13, bf16[256,512]{1,0:T(8,128)(2,1)} %bitcast.12, bf16[256,1024]{1,0:T(8,128)(2,1)} %bitcast.11, bf16[256,1024]{1,0:T(8,128)(2,1)} %oc_hbm.1, ...), custom_call_target="tpu_custom_call" | custom-call | tf_op jit(solution)/shard_map/pallas_call | solution.py:373
  125.2 0.0 copy-start
  125.2 1.9 %copy.11 = bf16[1,256,1024]{2,1,0:T(8,128)(2,1)} copy(bf16[1,256,1024]{2,1,0:T(8,128)(2,1)} %bitcast.9) | data formatting | bytes 1048576
  127.1 0.0 copy-done
  127.1 0.8 copy.12
Async XLA Ops:
  125.2 1.9 %copy-start = (bf16[256,1024]{1,0:T(8,128)(2,1)S(1)}, bf16[256,1024]{1,0:T(8,128)(2,1)}, u32[]{:S(2)}) copy-start(bf16[256,1024]{1,0:T(8,128)(2,1)} %get-tuple-element.5) | copy-start | bytes 1572868

commit v4 on v3

--- a/solution.py
+++ b/solution.py
@@ -9,7 +9,7 @@
 epsilon = 1e-05
 SEQ = ("z", "xh")
 Z = 8
-CHUNKS = 4
+CHUNKS = 8
 KV_CHUNKS = 4
 F32, BF16 = jnp.float32, jnp.bfloat16
 
@@ -26,16 +26,16 @@
 
 
 def kernel(
-    li_hbm, gain_hbm, cot_hbm, kvw_hbm, mlp_hbm, oc_hbm, wo_hbm, attn_out, ig_out,
-    li, gain, mlp, oc, cotb, wz, wk, pair, wo, own_terms, their_terms, tin, give,
+    li_hbm, gain_hbm, cot_hbm, kvw_hbm, mlp_hbm, oc_hbm, wo_hbm, attn_out, ig_hbm,
+    attn, ig_out,    li, gain, mlp, oc, cotb, wz, wk, pair, wo, own_terms, their_terms, tin, give,
     far_in, keep_in, rest_in, stat, coef, acc, pout, pin,
-    kv_s, kv_r, a2a_s, a2a_r, cot_s, cot_r, gr_s, gr_r, st_s, st_r, wo_s, wo_r, one_s, one_r, out_s, out_r, loc,
+    kv_s, kv_r, a2a_s, a2a_r, cot_s, cot_r, gr_s, gr_r, st_s, st_r, wo_s, wo_r, one_s, one_r, out_s, out_r, loc, res,
 ):
     s, z = lax.axis_index("section"), lax.axis_index("z")
     h, t = lax.axis_index("xh"), lax.axis_index("tp")
     hp = 1 - h
     y, c = t // 2, t % 2
-    zr, zl = (z + 1) % Z, (z + Z - 1) % Z
+    zr, zl, far = (z + 1) % Z, (z + Z - 1) % Z, (z + 4) % Z
     yr, yl, yo = [((y + i) % 4) * 2 + c for i in (1, 3, 2)]
     core, yr_c, yl_c, yo_c = [i + 1 - 2 * c for i in (t, yr, yl, yo)]
     mine = pl.ds(pl.multiple_of(h * 512, 512), 512)
@@ -47,7 +47,8 @@
     ]
     cot_own = pltpu.make_async_copy(cot_hbm, cotb.at[t, h], loc.at[4])
     wo_own = pltpu.make_async_copy(wo_hbm, wo.at[z], loc.at[5])
-    for load in [cot_own] + loads + [wo_own]:
+    kv_own = pltpu.make_async_copy(kvw_hbm, wz.at[z], loc.at[6])
+    for load in [cot_own, kv_own] + loads + [wo_own]:
         load.start()
 
     barrier = pltpu.get_barrier_semaphore()
@@ -113,7 +114,8 @@
     kv_part = [pl.ds(j * kv_rows, kv_rows) for j in range(KV_CHUNKS)]
 
     def kv_start(j):
-        ring_start(kvw_hbm.at[kv_part[j]], lambda i: wz.at[i, kv_part[j]], kv_s.at[j], kv_r.at[j])
+        own = kvw_hbm.at[kv_part[j]]
+        ring_start(own, lambda i: wz.at[i, kv_part[j]], kv_s.at[j], kv_r.at[j])
 
     def kv_step(k, j):
         ring_step(k, lambda i: wz.at[i, kv_part[j]], kv_rows, kv_s.at[j], kv_r.at[j])
@@ -122,31 +124,77 @@
         land = wk.at[t, kv_part[j]]
         for i in range(1, Z):
             zz = (t + i) % Z
-            pl.when(zz != z)(
-                rcopy(wz.at[zz, kv_part[j]], land, a2a_s.at[j, i], a2a_r.at[j, t], tp=zz).start
-            )
-            pl.when(zz == z)(
-                rcopy(kvw_hbm.at[kv_part[j]], land, a2a_s.at[j, i], a2a_r.at[j, t], tp=zz).start
-            )
-            sent.append(rcopy(wz.at[zz, kv_part[j]], land, a2a_s.at[j, i], a2a_r.at[j, t], tp=zz).wait_send)
-        pl.when(t != z)(pltpu.make_async_copy(wz.at[t, kv_part[j]], land, a2a_r.at[j, t]).start)
-        pl.when(t == z)(pltpu.make_async_copy(kvw_hbm.at[kv_part[j]], land, a2a_r.at[j, t]).start)
+            send(wz.at[zz, kv_part[j]], land, a2a_s.at[j, i], a2a_r.at[j, t], tp=zz)
+        pltpu.make_async_copy(wz.at[t, kv_part[j]], land, a2a_r.at[j, t]).start()
+
+    def kv_arrived(j, i):
+        arrived(wk.at[i, kv_part[j]], a2a_r.at[j, i])
 
     wo_rows = 1024 // CHUNKS
     wo_part = [pl.ds(j * wo_rows, wo_rows) for j in range(CHUNKS)]
 
-    def wo_step(k, j):
+    def wo_start(j):
+        ring_start(wo_hbm.at[wo_part[j]], lambda i: wo.at[i, wo_part[j]], wo_s.at[j], wo_r.at[j])
+
+    def wo_piece(k, j):
         ring_step(k, lambda i: wo.at[i, wo_part[j]], wo_rows, wo_s.at[j], wo_r.at[j])
 
+    def wo_step(k, quarter):
+        for j in range(quarter * CHUNKS // 4, (quarter + 1) * CHUNKS // 4):
+            wo_piece(k, j)
+
     cot_whole, cot_lower, cot_upper = lambda i: cotb.at[i], lambda i: cotb.at[i, 0], lambda i: cotb.at[i, 1]
 
-    half_kv = KV_CHUNKS // 2
-    group_a, group_b = range(half_kv), range(half_kv, KV_CHUNKS)
-    for j in group_a:
-        kv_start(j)
+    kv_start(0)
+    kv_start(1)
+    cot_own.wait()
     send(cot_hbm, cotb.at[t, h], one_s.at[0], one_r.at[0], xh=hp)
     for load in loads:
         load.wait()
+
+    @pl.when(s == 1)
+    def _():
+        @pl.loop(0, 8)
+        def _(i):
+            rows = pl.ds(pl.multiple_of(i * 32, 32), 32)
+            give[rows, :] = (oc[rows, other].astype(F32) + mlp[rows, other].astype(F32)).astype(BF16)
+
+    @pl.when(s == 0)
+    def _():
+        give[...] = mlp[:, other]
+
+    send(give, pair.at[t, h], one_s.at[3], one_r.at[3], xh=hp)
+    kv_step(1, 0)
+    kv_step(1, 1)
+    kv_start(2)
+    arrived(cotb.at[t, hp], one_r.at[0])
+    swap_start(cot_whole, cot_s, cot_r)
+    kv_step(2, 0)
+    kv_step(2, 1)
+    kv_step(1, 2)
+    kv_step(3, 0)
+    kv_step(3, 1)
+    kv_start(3)
+    swap_near(cot_whole, cot_lower, cot_upper, cot_s, cot_r)
+    kv_step(2, 2)
+    kv_own.wait()
+    kv_step(4, 0)
+    pass_on(0)
+    kv_step(4, 1)
+    pass_on(1)
+    kv_step(1, 3)
+    wo_start(0)
+    kv_step(3, 2)
+    swap_far(cot_whole, cot_lower, cot_upper, cot_s, cot_r)
+    kv_step(2, 3)
+    wo_start(1)
+    kv_step(4, 2)
+    pass_on(2)
+    kv_step(3, 3)
+    for j in range(2, CHUNKS):
+        wo_start(j)
+    kv_step(4, 3)
+    pass_on(3)
 
     @pl.when(s == 1)
     def _():
@@ -154,23 +202,6 @@
         def _(i):
             rows = pl.ds(pl.multiple_of(i * 32, 32), 32)
             pair[t, h, rows, :] = (oc[rows, mine].astype(F32) + mlp[rows, mine].astype(F32)).astype(BF16)
-            give[rows, :] = (oc[rows, other].astype(F32) + mlp[rows, other].astype(F32)).astype(BF16)
-
-    @pl.when(s == 0)
-    def _():
-        give[...] = mlp[:, other]
-
-    send(give, pair.at[t, h], one_s.at[3], one_r.at[3], xh=hp)
-    cot_own.wait()
-    arrived(cotb.at[t, hp], one_r.at[0])
-    swap_start(cot_whole, cot_s, cot_r)
-    for k in (1, 2):
-        for j in group_a:
-            kv_step(k, j)
-    for j in group_b:
-        kv_start(j)
-    for j in group_a:
-        kv_step(3, j)
 
     @pl.loop(0, 8)
     def _(i):
@@ -178,25 +209,10 @@
         v = li[rows, :].astype(F32)
         coef[rows, :] = jnp.broadcast_to(jnp.sum(v * v, axis=1, keepdims=True), (32, 128))
 
-    swap_near(cot_whole, cot_lower, cot_upper, cot_s, cot_r)
-    for j in group_a:
-        kv_step(4, j)
-        pass_on(j)
-    for j in group_b:
-        kv_step(1, j)
-    swap_far(cot_whole, cot_lower, cot_upper, cot_s, cot_r)
-    for k in (2, 3):
-        for j in group_b:
-            kv_step(k, j)
-    for j in range(CHUNKS):
-        ring_start(wo_hbm.at[wo_part[j]], lambda i: wo.at[i, wo_part[j]], wo_s.at[j], wo_r.at[j])
-    for j in group_b:
-        kv_step(4, j)
-        pass_on(j)
     swap_end(cot_whole, cot_r)
     for j in range(KV_CHUNKS):
         for i in range(Z):
-            arrived(wk.at[i, kv_part[j]], a2a_r.at[j, i])
+            kv_arrived(j, i)
 
     def terms(half, into):
         into[...] = jnp.dot(cotb[0, half], wk[0], preferred_element_type=F32)
@@ -246,48 +262,57 @@
             - li[rows, columns].astype(F32) * coef[rows, 1:2]
         )
 
-    to_far = rcopy(ig_out.at[:, other], far_in, one_s.at[2], one_r.at[2], section=1 - s, xh=hp)
+    top, bottom = pl.ds(0, 128), pl.ds(128, 128)
+    ig_done = pltpu.make_async_copy(ig_out, ig_hbm, res.at[4])
+    to_far = [
+        rcopy(ig_out.at[r, other], far_in.at[r], one_s.at[i], one_r.at[i], section=1 - s, xh=hp)
+        for i, r in ((2, top), (6, bottom))
+    ]
     to_keep = rcopy(ig_out.at[:, mine], keep_in, one_s.at[4], one_r.at[4], section=1 - s)
     to_rest = rcopy(ig_out.at[:, other], rest_in, one_s.at[5], one_r.at[5], section=1 - s)
-    for copy in (to_far, to_keep, to_rest):
+    for copy in to_far + [to_keep, to_rest]:
         sent.append(lambda copy=copy: pl.when(s == 1)(copy.wait_send))
 
     @pl.when(s == 1)
     def _():
-        def down(columns, terms_ref):
-            @pl.loop(0, 8)
+        def down(first, last, columns, terms_ref):
+            @pl.loop(first, last)
             def _(i):
                 rows = pl.ds(pl.multiple_of(i * 32, 32), 32)
                 grad = oc[rows, columns].astype(F32) + mlp[rows, columns].astype(F32)
                 ig_out[rows, columns] = (grad + norm_back(rows, columns, terms_ref)).astype(BF16)
 
-        down(other, tin)
-        to_far.start()
-        down(mine, own_terms)
+        down(0, 4, other, tin)
+        to_far[0].start()
+        down(4, 8, other, tin)
+        to_far[1].start()
+        down(0, 8, mine, own_terms)
         to_keep.start()
         to_rest.start()
+        ig_done.start()
 
     wo_step(1, 3)
     arrived(pair.at[t, hp], one_r.at[3])
 
-    def pair_refs(half):
-        return (
-            lambda i: pair.at[i, half], lambda i: pair.at[i, half, pl.ds(0, 128)],
-            lambda i: pair.at[i, half, pl.ds(128, 128)],
+    def pair_refs(half, first, rows):
+        return tuple(
+            lambda i, part=pl.ds(start, count): pair.at[i, half, part]
+            for start, count in ((first, rows), (first, rows // 2), (first + rows // 2, rows // 2))
         )
 
-    theirs, ours = pair_refs(hp), pair_refs(h)
-
-    @pl.when(s == 0)
-    def _():
-        arrived(far_in, one_r.at[2])
-
-        @pl.loop(0, 8)
-        def _(i):
-            rows = pl.ds(pl.multiple_of(i * 32, 32), 32)
-            pair[t, hp, rows, :] = (far_in[rows, :].astype(F32) + pair[t, hp, rows, :].astype(F32)).astype(BF16)
-
-    swap_start(theirs[0], gr_s.at[0], gr_r.at[0])
+    theirs, ours = [pair_refs(hp, 0, 128), pair_refs(hp, 128, 128)], pair_refs(h, 0, 256)
+
+    for n in (0, 1):
+        @pl.when(s == 0)
+        def _():
+            arrived(far_in.at[(top, bottom)[n]], one_r.at[(2, 6)[n]])
+
+            @pl.loop(4 * n, 4 * n + 4)
+            def _(i):
+                rows = pl.ds(pl.multiple_of(i * 32, 32), 32)
+                pair[t, hp, rows, :] = (far_in[rows, :].astype(F32) + pair[t, hp, rows, :].astype(F32)).astype(BF16)
+
+        swap_start(theirs[n][0], gr_s.at[n], gr_r.at[n])
 
     @pl.when(s == 0)
     def _():
@@ -298,11 +323,12 @@
             rows = pl.ds(pl.multiple_of(i * 32, 32), 32)
             pair[t, h, rows, :] = (keep_in[rows, :].astype(F32) + mlp[rows, mine].astype(F32)).astype(BF16)
 
-    swap_start(ours[0], gr_s.at[1], gr_r.at[1])
+    swap_start(ours[0], gr_s.at[2], gr_r.at[2])
 
     wo_step(2, 0)
     wo_step(2, 1)
-    swap_near(*theirs, gr_s.at[0], gr_r.at[0])
+    for n in (0, 1):
+        swap_near(*theirs[n], gr_s.at[n], gr_r.at[n])
     wo_step(2, 2)
 
     @pl.when(s == 0)
@@ -318,12 +344,15 @@
 
         up(mine, own_terms, keep_in)
         up(other, tin, rest_in)
-
-    swap_near(*ours, gr_s.at[1], gr_r.at[1])
-    swap_far(*theirs, gr_s.at[0], gr_r.at[0])
+        ig_done.start()
+
+    for n in (0, 1):
+        swap_far(*theirs[n], gr_s.at[n], gr_r.at[n])
+    swap_near(*ours, gr_s.at[2], gr_r.at[2])
     wo_step(2, 3)
-    swap_far(*ours, gr_s.at[1], gr_r.at[1])
-    swap_end(theirs[0], gr_r.at[0])
+    swap_far(*ours, gr_s.at[2], gr_r.at[2])
+    for n in (0, 1):
+        swap_end(theirs[n][0], gr_r.at[n])
     wo_own.wait()
     wo_step(3, 0)
 
@@ -345,37 +374,45 @@
 
     first_blocks(hp)
     wo_step(3, 1)
-    swap_end(ours[0], gr_r.at[1])
+    swap_end(ours[0], gr_r.at[2])
     first_blocks(h)
+    for n in range(4):
+        if n > 1:
+            wo_step(3, n)
+        columns = pl.ds(n * 256, 256)
+        for half in (hp, h):
+            acc[half, :, columns] += product(half, (z + 3) % Z, columns) + product(half, (z + Z - 3) % Z, columns)
     for j in range(CHUNKS):
-        if j > 1:
-            wo_step(3, j)
-        for half in (hp, h):
-            acc[half, :, wo_part[j]] += product(half, (z + 3) % Z, wo_part[j]) + product(
-                half, (z + Z - 3) % Z, wo_part[j]
-            )
-    for j in range(CHUNKS):
-        wo_step(4, j)
-        far = (z + 4) % Z
+        wo_piece(4, j)
         pout[j] = (acc[hp, :, wo_part[j]] + product(hp, far, wo_part[j])).astype(BF16)
         send(pout.at[j], pin.at[j], out_s.at[j], out_r.at[j], xh=hp)
         acc[h, :, wo_part[j]] += product(h, far, wo_part[j])
+    results = []
     for j in range(CHUNKS):
         arrived(pin.at[j], out_r.at[j])
-        attn_out[:, wo_part[j]] = (acc[h, :, wo_part[j]] + pin[j].astype(F32)).astype(BF16)
+        attn[:, wo_part[j]] = (acc[h, :, wo_part[j]] + pin[j].astype(F32)).astype(BF16)
+        if j % 2:
+            columns = pl.ds((j - 1) * wo_rows, 2 * wo_rows)
+            results.append(pltpu.make_async_copy(attn.at[:, columns], attn_out.at[:, columns], res.at[j // 2]))
+            results[-1].start()
+    for result in results:
+        result.wait()
+    ig_done.wait()
     finish()
 
 
 def body(layer_input, norm_gain, kv_cotangent, kv_weight, mlp_grads, output_cotangent, out_weight):
-    vmem, hbm = pl.BlockSpec(memory_space=pltpu.VMEM), pl.BlockSpec(memory_space=pltpu.HBM)
+    hbm = pl.BlockSpec(memory_space=pltpu.HBM)
     dma = lambda *n: pltpu.SemaphoreType.DMA(n)
     out = jax.ShapeDtypeStruct((256, 1024), BF16)
     attn, grads = pl.pallas_call(
         kernel,
         out_shape=(out, out),
         in_specs=[hbm] * 7,
-        out_specs=(vmem, vmem),
+        out_specs=(hbm, hbm),
         scratch_shapes=[
+            pltpu.VMEM((256, 1024), BF16),
+            pltpu.VMEM((256, 1024), BF16),
             pltpu.VMEM((256, 1024), BF16),
             pltpu.VMEM((1, 1024), F32),
             pltpu.VMEM((256, 1024), BF16),
@@ -400,12 +437,13 @@
             dma(KV_CHUNKS, 8), dma(KV_CHUNKS, 8),
             dma(KV_CHUNKS, 8), dma(KV_CHUNKS, 8),
             dma(8), dma(8),
-            dma(2, 8), dma(2, 8),
+            dma(3, 8), dma(3, 8),
             dma(8), dma(8),
             dma(CHUNKS, 8), dma(CHUNKS, 8),
-            dma(6), dma(6),
+            dma(7), dma(7),
             dma(CHUNKS), dma(CHUNKS),
-            dma(6),
+            dma(7),
+            dma(5),
         ],
         compiler_params=pltpu.CompilerParams(
             collective_id=0, has_side_effects=True, vmem_limit_bytes=58 * 2**20

time: 128 us -> 124 us (0.969)
  Pallas kernels: 125 us -> 119 us
    pallas_call x1, Pallas kernels: 125 us -> 119 us  [body(): pl.pallas_call(kernel, out_shape=(out, out), in_specs=[hbm] * 7, out_spec...]
where the time goes in v4:
time: 124 us; the launch traced here: 123 us
  Pallas kernels  119 us (96%)
  local copies, waits for them, and re-layouts  2.72 us (2%)
    pallas_call x1, Pallas kernels, body(): pl.pallas_call(kernel, out_shape=(out, out), in_specs=[hbm] * 7, out_spec...  119 us
    unnamed x4, local copies, waits for them, and re-layouts  2.72 us

profile of v4, /device:TPU:2, one launch (start us, length us, event | category | flops | bytes accessed | tf_op | source)
XLA Modules:
  0.0 122.7 jit_solution(1087929532801626370)
XLA Ops:
  0.6 119.3 %shard_map.86 = (bf16[256,1024]{1,0:T(8,128)(2,1)}, bf16[256,1024]{1,0:T(8,128)(2,1)}) custom-call(bf16[256,1024]{1,0:T(8,128)(2,1)} %bitcast.10, f32[1,1024]{1,0:T(1,128)} %gain_hbm.1, bf16[256,256]{1,0:T(8,128)(2,1)} %bitcast.13, bf16[256,512]{1,0:T(8,128)(2,1)} %bitcast.12, bf16[256,1024]{1,0:T(8,128)(2,1)} %bitcast.11, bf16[256,1024]{1,0:T(8,128)(2,1)} %oc_hbm.1, ...), custom_call_target="tpu_custom_call" | custom-call | tf_op jit(solution)/shard_map/pallas_call | solution.py:408
  119.9 0.0 copy-start
  120.0 1.9 %copy.11 = bf16[1,256,1024]{2,1,0:T(8,128)(2,1)} copy(bf16[1,256,1024]{2,1,0:T(8,128)(2,1)} %bitcast.9) | data formatting | bytes 1048576
  121.9 0.0 copy-done
  121.9 0.8 copy.12
Async XLA Ops:
  119.9 1.9 %copy-start = (bf16[256,1024]{1,0:T(8,128)(2,1)S(1)}, bf16[256,1024]{1,0:T(8,128)(2,1)}, u32[]{:S(2)}) copy-start(bf16[256,1024]{1,0:T(8,128)(2,1)} %get-tuple-element.5) | copy-start | bytes 1572868

commit v5 on v4

--- a/solution.py
+++ b/solution.py
@@ -26,11 +26,12 @@
 
 
 def kernel(
-    li_hbm, gain_hbm, cot_hbm, kvw_hbm, mlp_hbm, oc_hbm, wo_hbm, attn_out, ig_hbm,
-    attn, ig_out,    li, gain, mlp, oc, cotb, wz, wk, pair, wo, own_terms, their_terms, tin, give,
+    li_hbm, gain_hbm, cot_hbm, kvw_hbm, mlp_hbm, oc_hbm, wo_hbm, result,
+       li, gain, mlp, oc, cotb, wz, wk, pair, wo, own_terms, their_terms, tin, give,
     far_in, keep_in, rest_in, stat, coef, acc, pout, pin,
-    kv_s, kv_r, a2a_s, a2a_r, cot_s, cot_r, gr_s, gr_r, st_s, st_r, wo_s, wo_r, one_s, one_r, out_s, out_r, loc, res,
+    kv_s, kv_r, a2a_s, a2a_r, cot_s, cot_r, gr_s, gr_r, st_s, st_r, wo_s, wo_r, one_s, one_r, out_s, out_r, loc,
 ):
+    attn, ig_out = result.at[0], result.at[1]
     s, z = lax.axis_index("section"), lax.axis_index("z")
     h, t = lax.axis_index("xh"), lax.axis_index("tp")
     hp = 1 - h
@@ -41,6 +42,12 @@
     mine = pl.ds(pl.multiple_of(h * 512, 512), 512)
     other = pl.ds(pl.multiple_of(hp * 512, 512), 512)
 
+    barrier = pltpu.get_barrier_semaphore()
+    greet = [{"xh": hp}, {"section": 1 - s}, {"section": 1 - s, "xh": hp}, {"z": zr}, {"z": zl}]
+    greet += [{"tp": (t + i) % Z} for i in range(1, Z)]
+    for to in greet:
+        pl.semaphore_signal(barrier, inc=1, device_id=to, device_id_type=pl.DeviceIdType.MESH)
+
     loads = [
         pltpu.make_async_copy(src, dst, loc.at[i])
         for i, (src, dst) in enumerate(((li_hbm, li), (gain_hbm, gain), (mlp_hbm, mlp), (oc_hbm, oc)))
@@ -51,38 +58,34 @@
     for load in [cot_own, kv_own] + loads + [wo_own]:
         load.start()
 
-    barrier = pltpu.get_barrier_semaphore()
-    greet = [{"xh": hp}, {"section": 1 - s}, {"section": 1 - s, "xh": hp}, {"z": zr}, {"z": zl}]
-    greet += [{"tp": (t + i) % Z} for i in range(1, Z)]
-    for to in greet:
-        pl.semaphore_signal(barrier, inc=1, device_id=to, device_id_type=pl.DeviceIdType.MESH)
     pl.semaphore_wait(barrier, len(greet))
 
     sent = []
 
-    def send(src, dst, send_sem, recv_sem, **to):
+    def send(src, dst, send_sem, recv_sem, log=sent, **to):
         copy = rcopy(src, dst, send_sem, recv_sem, **to)
         copy.start()
-        sent.append(copy.wait_send)
+        log.append(copy.wait_send)
 
     def finish():
         for wait in sent:
             wait()
-
-    def ring_start(own, slot, ss, rs):
-        send(own, slot(z), ss.at[0], rs.at[0], z=zr)
-        send(own, slot(z), ss.at[4], rs.at[4], z=zl)
-
-    def ring_step(k, slot, rows, ss, rs):
+        sent.clear()
+
+    def ring_start(own, slot, ss, rs, log=sent):
+        send(own, slot(z), ss.at[0], rs.at[0], log, z=zr)
+        send(own, slot(z), ss.at[4], rs.at[4], log, z=zl)
+
+    def ring_step(k, slot, rows, ss, rs, log=sent):
         a, b = (z + Z - k) % Z, (z + k) % Z
         first, last = pl.ds(0, rows // 2), pl.ds(rows // 2, rows // 2)
         if k < 4:
             arrived(slot(a), rs.at[k - 1])
             part = slot(a) if k < 3 else slot(a).at[first]
-            send(part, part, ss.at[k], rs.at[k], z=zr)
+            send(part, part, ss.at[k], rs.at[k], log, z=zr)
             arrived(slot(b), rs.at[k + 3])
             part = slot(b) if k < 3 else slot(b).at[last]
-            send(part, part, ss.at[k + 4], rs.at[k + 4], z=zl)
+            send(part, part, ss.at[k + 4], rs.at[k + 4], log, z=zl)
         else:
             arrived(slot(a).at[first], rs.at[3])
             arrived(slot(a).at[last], rs.at[7])
@@ -133,11 +136,13 @@
     wo_rows = 1024 // CHUNKS
     wo_part = [pl.ds(j * wo_rows, wo_rows) for j in range(CHUNKS)]
 
+    wo_sent = [[] for _ in range(CHUNKS)]
+
     def wo_start(j):
-        ring_start(wo_hbm.at[wo_part[j]], lambda i: wo.at[i, wo_part[j]], wo_s.at[j], wo_r.at[j])
+        ring_start(wo_hbm.at[wo_part[j]], lambda i: wo.at[i, wo_part[j]], wo_s.at[j], wo_r.at[j], wo_sent[j])
 
     def wo_piece(k, j):
-        ring_step(k, lambda i: wo.at[i, wo_part[j]], wo_rows, wo_s.at[j], wo_r.at[j])
+        ring_step(k, lambda i: wo.at[i, wo_part[j]], wo_rows, wo_s.at[j], wo_r.at[j], wo_sent[j])
 
     def wo_step(k, quarter):
         for j in range(quarter * CHUNKS // 4, (quarter + 1) * CHUNKS // 4):
@@ -177,21 +182,22 @@
     kv_start(3)
     swap_near(cot_whole, cot_lower, cot_upper, cot_s, cot_r)
     kv_step(2, 2)
+    wo_start(0)
     kv_own.wait()
     kv_step(4, 0)
     pass_on(0)
     kv_step(4, 1)
     pass_on(1)
     kv_step(1, 3)
-    wo_start(0)
+    wo_start(1)
     kv_step(3, 2)
     swap_far(cot_whole, cot_lower, cot_upper, cot_s, cot_r)
     kv_step(2, 3)
-    wo_start(1)
+    wo_start(2)
     kv_step(4, 2)
     pass_on(2)
     kv_step(3, 3)
-    for j in range(2, CHUNKS):
+    for j in range(3, CHUNKS):
         wo_start(j)
     kv_step(4, 3)
     pass_on(3)
@@ -263,7 +269,6 @@
         )
 
     top, bottom = pl.ds(0, 128), pl.ds(128, 128)
-    ig_done = pltpu.make_async_copy(ig_out, ig_hbm, res.at[4])
     to_far = [
         rcopy(ig_out.at[r, other], far_in.at[r], one_s.at[i], one_r.at[i], section=1 - s, xh=hp)
         for i, r in ((2, top), (6, bottom))
@@ -289,7 +294,6 @@
         down(0, 8, mine, own_terms)
         to_keep.start()
         to_rest.start()
-        ig_done.start()
 
     wo_step(1, 3)
     arrived(pair.at[t, hp], one_r.at[3])
@@ -344,7 +348,6 @@
 
         up(mine, own_terms, keep_in)
         up(other, tin, rest_in)
-        ig_done.start()
 
     for n in (0, 1):
         swap_far(*theirs[n], gr_s.at[n], gr_r.at[n])
@@ -382,22 +385,17 @@
         columns = pl.ds(n * 256, 256)
         for half in (hp, h):
             acc[half, :, columns] += product(half, (z + 3) % Z, columns) + product(half, (z + Z - 3) % Z, columns)
+    finish()
     for j in range(CHUNKS):
         wo_piece(4, j)
         pout[j] = (acc[hp, :, wo_part[j]] + product(hp, far, wo_part[j])).astype(BF16)
         send(pout.at[j], pin.at[j], out_s.at[j], out_r.at[j], xh=hp)
         acc[h, :, wo_part[j]] += product(h, far, wo_part[j])
-    results = []
+        for wait in wo_sent[j]:
+            wait()
     for j in range(CHUNKS):
         arrived(pin.at[j], out_r.at[j])
         attn[:, wo_part[j]] = (acc[h, :, wo_part[j]] + pin[j].astype(F32)).astype(BF16)
-        if j % 2:
-            columns = pl.ds((j - 1) * wo_rows, 2 * wo_rows)
-            results.append(pltpu.make_async_copy(attn.at[:, columns], attn_out.at[:, columns], res.at[j // 2]))
-            results[-1].start()
-    for result in results:
-        result.wait()
-    ig_done.wait()
     finish()
 
 
@@ -405,14 +403,12 @@
     hbm = pl.BlockSpec(memory_space=pltpu.HBM)
     dma = lambda *n: pltpu.SemaphoreType.DMA(n)
     out = jax.ShapeDtypeStruct((256, 1024), BF16)
-    attn, grads = pl.pallas_call(
+    result = pl.pallas_call(
         kernel,
-        out_shape=(out, out),
+        out_shape=pltpu.VMEM((2, 256, 1024), BF16),
         in_specs=[hbm] * 7,
-        out_specs=(hbm, hbm),
+        out_specs=pl.BlockSpec(memory_space=pltpu.VMEM),
         scratch_shapes=[
-            pltpu.VMEM((256, 1024), BF16),
-            pltpu.VMEM((256, 1024), BF16),
             pltpu.VMEM((256, 1024), BF16),
             pltpu.VMEM((1, 1024), F32),
             pltpu.VMEM((256, 1024), BF16),
@@ -443,7 +439,6 @@
             dma(7), dma(7),
             dma(CHUNKS), dma(CHUNKS),
             dma(7),
-            dma(5),
         ],
         compiler_params=pltpu.CompilerParams(
             collective_id=0, has_side_effects=True, vmem_limit_bytes=58 * 2**20
@@ -452,7 +447,7 @@
         layer_input[0], norm_gain, kv_cotangent[0], kv_weight[0],
         mlp_grads[0], output_cotangent, out_weight[0],
     )
-    return attn[None], grads[None]
+    return result[:1], result[1:]
 
 
 def solution(mesh):

time: 124 us -> 120 us (0.968)
  local copies, waits for them, and re-layouts: 2.72 us -> 1.03 us
    unnamed x4 -> x0, local copies, waits for them, and re-layouts: 2.72 us -> none
    pallas_call x1, Pallas kernels: 119 us -> 118 us  [body(): pl.pallas_call(kernel, out_shape=pltpu.VMEM((2, 256, 1024), BF16), in_spe...]
where the time goes in v5:
time: 120 us
  Pallas kernels  118 us (98%)
    pallas_call x1, Pallas kernels, body(): pl.pallas_call(kernel, out_shape=pltpu.VMEM((2, 256, 1024), BF16), in_spe...  118 us

profile of v5, /device:TPU:2, one launch (start us, length us, event | category | flops | bytes accessed | tf_op | source)
XLA Modules:
  0.0 119.7 jit_solution(10321135076959712384)
XLA Ops:
  0.6 118.0 %shard_map.86 = bf16[2,256,1024]{2,1,0:T(8,128)(2,1)S(1)} custom-call(bf16[256,1024]{1,0:T(8,128)(2,1)} %bitcast.6, f32[1,1024]{1,0:T(1,128)} %gain_hbm.1, bf16[256,256]{1,0:T(8,128)(2,1)} %bitcast.9, bf16[256,512]{1,0:T(8,128)(2,1)} %bitcast.8, bf16[256,1024]{1,0:T(8,128)(2,1)} %bitcast.7, bf16[256,1024]{1,0:T(8,128)(2,1)} %oc_hbm.1, bf16[1024,512]{1,0:T(8,128)(2,1)} %bitcast.5), custom_call_target="tpu_custom_call" | custom-call | tf_op jit(solution)/shard_map/pallas_call | solution.py:406
  118.7 1.0 fusion

commit v6 on v5

--- a/solution.py
+++ b/solution.py
@@ -183,24 +183,27 @@
     swap_near(cot_whole, cot_lower, cot_upper, cot_s, cot_r)
     kv_step(2, 2)
     wo_start(0)
+    wo_start(1)
     kv_own.wait()
     kv_step(4, 0)
     pass_on(0)
     kv_step(4, 1)
     pass_on(1)
     kv_step(1, 3)
-    wo_start(1)
+    wo_start(2)
     kv_step(3, 2)
     swap_far(cot_whole, cot_lower, cot_upper, cot_s, cot_r)
     kv_step(2, 3)
-    wo_start(2)
+    wo_start(3)
+    wo_start(4)
     kv_step(4, 2)
     pass_on(2)
     kv_step(3, 3)
-    for j in range(3, CHUNKS):
+    for j in range(5, CHUNKS):
         wo_start(j)
     kv_step(4, 3)
     pass_on(3)
+    wo_step(1, 0)
 
     @pl.when(s == 1)
     def _():
@@ -215,40 +218,48 @@
         v = li[rows, :].astype(F32)
         coef[rows, :] = jnp.broadcast_to(jnp.sum(v * v, axis=1, keepdims=True), (32, 128))
 
+    wo_step(1, 1)
     swap_end(cot_whole, cot_r)
     for j in range(KV_CHUNKS):
         for i in range(Z):
             kv_arrived(j, i)
 
-    def terms(half, into):
-        into[...] = jnp.dot(cotb[0, half], wk[0], preferred_element_type=F32)
-
-        @pl.loop(1, Z)
+    def terms(half, columns):
+        total = jnp.dot(cotb[0, half], wk[0, :, columns], preferred_element_type=F32)
+        for i in range(1, Z):
+            total += jnp.dot(cotb[i, half], wk[i, :, columns], preferred_element_type=F32)
+        return total
+
+    for n, columns in enumerate((pl.ds(0, 256), pl.ds(256, 256))):
+        their_terms[:, columns] = terms(hp, columns).astype(BF16)
+        index = (1, 7)[n]
+        send(their_terms.at[:, columns], tin.at[:, columns], one_s.at[index], one_r.at[index], xh=hp)
+    wo_step(1, 2)
+    for columns in (pl.ds(0, 256), pl.ds(256, 256)):
+        own_terms[:, columns] = terms(h, columns)
+    lane = lax.broadcasted_iota(jnp.int32, (32, 128), 1)
+
+    def inner(columns, terms_ref, so_far):
+        @pl.loop(0, 8)
         def _(i):
-            into[...] += jnp.dot(cotb[i, half], wk[i], preferred_element_type=F32)
-
-    terms(hp, own_terms)
-    their_terms[...] = own_terms[...].astype(BF16)
-    send(their_terms, tin, one_s.at[1], one_r.at[1], xh=hp)
-    wo_step(1, 0)
-    terms(h, own_terms)
-    lane = lax.broadcasted_iota(jnp.int32, (32, 128), 1)
-    wo_step(1, 1)
-    arrived(tin, one_r.at[1])
-
-    @pl.loop(0, 8)
-    def _(i):
-        rows = pl.ds(pl.multiple_of(i * 32, 32), 32)
-        inner = jnp.sum(gain[:, mine] * own_terms[rows, :] * li[rows, mine].astype(F32), axis=1, keepdims=True)
-        inner += jnp.sum(
-            gain[:, other] * tin[rows, :].astype(F32) * li[rows, other].astype(F32), axis=1, keepdims=True
-        )
-        coef[rows, :] = jnp.where(lane == 0, coef[rows, :], jnp.broadcast_to(inner, (32, 128)))
-
+            rows = pl.ds(pl.multiple_of(i * 32, 32), 32)
+            part = jnp.sum(
+                gain[:, columns] * terms_ref[rows, :].astype(F32) * li[rows, columns].astype(F32),
+                axis=1, keepdims=True,
+            )
+            if so_far:
+                part += coef[rows, 1:2]
+            coef[rows, :] = jnp.where(lane == 0, coef[rows, :], jnp.broadcast_to(part, (32, 128)))
+
+    inner(mine, own_terms, False)
+    wo_step(1, 3)
+    for columns, index in ((pl.ds(0, 256), 1), (pl.ds(256, 256), 7)):
+        arrived(tin.at[:, columns], one_r.at[index])
+
+    inner(other, tin, True)
     stat[t] = coef[...].T[:8]
     for i in range(1, Z):
         send(stat.at[t], stat.at[t], st_s.at[i], st_r.at[t], tp=(t + i) % Z)
-    wo_step(1, 2)
     for i in range(1, Z):
         place = (t + i) % Z
         arrived(stat.at[place], st_r.at[place])
@@ -295,7 +306,7 @@
         to_keep.start()
         to_rest.start()
 
-    wo_step(1, 3)
+    wo_step(2, 0)
     arrived(pair.at[t, hp], one_r.at[3])
 
     def pair_refs(half, first, rows):
@@ -329,7 +340,6 @@
 
     swap_start(ours[0], gr_s.at[2], gr_r.at[2])
 
-    wo_step(2, 0)
     wo_step(2, 1)
     for n in (0, 1):
         swap_near(*theirs[n], gr_s.at[n], gr_r.at[n])
@@ -436,7 +446,7 @@
             dma(3, 8), dma(3, 8),
             dma(8), dma(8),
             dma(CHUNKS, 8), dma(CHUNKS, 8),
-            dma(7), dma(7),
+            dma(8), dma(8),
             dma(CHUNKS), dma(CHUNKS),
             dma(7),
         ],

time: 120 us -> 120 us (level)
  no operation moved by 1% of the time
where the time goes in v6:
time: 120 us
  Pallas kernels  118 us (98%)
    pallas_call x1, Pallas kernels, body(): pl.pallas_call(kernel, out_shape=pltpu.VMEM((2, 256, 1024), BF16), in_spe...  118 us

profile of v6, /device:TPU:2, one launch (start us, length us, event | category | flops | bytes accessed | tf_op | source)
XLA Modules:
  0.0 119.7 jit_solution(8142690002425805335)
XLA Ops:
  0.6 118.0 %shard_map.86 = bf16[2,256,1024]{2,1,0:T(8,128)(2,1)S(1)} custom-call(bf16[256,1024]{1,0:T(8,128)(2,1)} %bitcast.6, f32[1,1024]{1,0:T(1,128)} %gain_hbm.1, bf16[256,256]{1,0:T(8,128)(2,1)} %bitcast.9, bf16[256,512]{1,0:T(8,128)(2,1)} %bitcast.8, bf16[256,1024]{1,0:T(8,128)(2,1)} %bitcast.7, bf16[256,1024]{1,0:T(8,128)(2,1)} %oc_hbm.1, bf16[1024,512]{1,0:T(8,128)(2,1)} %bitcast.5), custom_call_target="tpu_custom_call" | custom-call | tf_op jit(solution)/shard_map/pallas_call | solution.py:416
  118.7 1.0 fusion

commit v7 on v6

--- a/solution.py
+++ b/solution.py
@@ -287,7 +287,7 @@
     to_keep = rcopy(ig_out.at[:, mine], keep_in, one_s.at[4], one_r.at[4], section=1 - s)
     to_rest = rcopy(ig_out.at[:, other], rest_in, one_s.at[5], one_r.at[5], section=1 - s)
     for copy in to_far + [to_keep, to_rest]:
-        sent.append(lambda copy=copy: pl.when(s == 1)(copy.wait_send))
+        wo_sent[0].append(lambda copy=copy: pl.when(s == 1)(copy.wait_send))
 
     @pl.when(s == 1)
     def _():
@@ -307,6 +307,7 @@
         to_rest.start()
 
     wo_step(2, 0)
+    finish()
     arrived(pair.at[t, hp], one_r.at[3])
 
     def pair_refs(half, first, rows):

time: 120 us -> 120 us (level)
  no operation moved by 1% of the time
where the time goes in v7:
time: 120 us
  Pallas kernels  118 us (98%)
    pallas_call x1, Pallas kernels, body(): pl.pallas_call(kernel, out_shape=pltpu.VMEM((2, 256, 1024), BF16), in_spe...  118 us

profile of v7, /device:TPU:2, one launch (start us, length us, event | category | flops | bytes accessed | tf_op | source)
XLA Modules:
  0.0 119.7 jit_solution(14413400723690576209)
XLA Ops:
  0.6 118.0 %shard_map.86 = bf16[2,256,1024]{2,1,0:T(8,128)(2,1)S(1)} custom-call(bf16[256,1024]{1,0:T(8,128)(2,1)} %bitcast.6, f32[1,1024]{1,0:T(1,128)} %gain_hbm.1, bf16[256,256]{1,0:T(8,128)(2,1)} %bitcast.9, bf16[256,512]{1,0:T(8,128)(2,1)} %bitcast.8, bf16[256,1024]{1,0:T(8,128)(2,1)} %bitcast.7, bf16[256,1024]{1,0:T(8,128)(2,1)} %oc_hbm.1, bf16[1024,512]{1,0:T(8,128)(2,1)} %bitcast.5), custom_call_target="tpu_custom_call" | custom-call | tf_op jit(solution)/shard_map/pallas_call | solution.py:417
  118.7 1.0 fusion
